TPU v7x, 512 devices: a whole 4x8x8 slice. The times are simulated.
512 devices in a mesh: sec: 32 (over x, z), strip: 16 (over y, core).
Axes of the slice: x: 4, y: 8, z: 8, core: 2. Of those that a mesh axis runs over, the one named last changes fastest.
Arguments:
- raw_image: bfloat16 [32, 512, 512], P('sec', 'strip'), may hold values from -6 to 6
- w_first: bfloat16 [9, 32], replicated, may hold values from -2 to 2
- gain_one: float32 [32], replicated, may hold values from 0.25 to 1.75
- w_second: bfloat16 [3, 32, 96], replicated, may hold values from -0.375 to 0.375
- gain_two: float32 [32], replicated, may hold values from 0.25 to 1.75
- offsets: int32 [32, 2], replicated, may hold values from -8 to 8, as said below
- w_third: bfloat16 [9, 32, 96], replicated, may hold values from -0.21875 to 0.21875
- w_fourth: bfloat16 [9, 32, 96], replicated, may hold values from -0.21875 to 0.21875
Outputs:
- volume_out: float32 [32, 32, 256, 256], P('sec', None, 'strip')
Inputs may be any that keep to these rules, and one draw needn't show every extreme that they name: `offsets`: every entry lies in -8 to 8; in both columns some section has exactly 8 and another exactly -8.
All inputs are finite; a program needn't handle non-finite values.
Results may differ from a plain program's by a relative error of at most 0.0051.
Values may be sent and summed in bfloat16 or wider, within the bound.
A program may use at most 64 MiB of HBM per device.

v0:
```python
import jax
import jax.numpy as jnp
import numpy as np
from jax import lax
from jax.sharding import PartitionSpec as P

OFF = 8


def from_behind(x, axis, by):
    peers = lax.axis_size(axis)
    pairs = [(i, i + by) for i in range(peers) if 0 <= i + by < peers]
    return lax.ppermute(x, axis, pairs)


def with_halo(block, sides, width):
    for axis, dim in sides:
        count = lax.axis_size(axis)
        forward = [(i, i + 1) for i in range(count - 1)]
        backward = [(target, source) for source, target in forward]
        low = lax.ppermute(
            lax.slice_in_dim(block, block.shape[dim] - width, None, axis=dim), axis, forward
        )
        high = lax.ppermute(lax.slice_in_dim(block, 0, width, axis=dim), axis, backward)
        block = jnp.concatenate([low, block, high], axis=dim)
    return block


def normalize(h, gain):
    v = jax.nn.silu(h)
    ms = jnp.mean(v * v, axis=1, keepdims=True)
    return v / jnp.sqrt(1.0 + ms) * gain[None, :, None, None]


def first_level(rows_pad, count, w_first, gain_one):
    breadth = rows_pad.shape[2] // 2
    colpad = jnp.pad(rows_pad, ((0, 0), (0, 0), (1, 1)))
    patches = []
    for tap_a in range(3):
        for tap_b in range(3):
            patches.append(
                colpad[:, tap_a : tap_a + 2 * count - 1 : 2, tap_b : tap_b + 2 * breadth - 1 : 2]
            )
    stacked = jnp.stack(patches, axis=1)
    first = jnp.einsum("tc,styx->scyx", w_first, stacked, preferred_element_type=jnp.float32)
    return normalize(first, gain_one).astype(jnp.bfloat16)


def second_level(level_ext, count, w_second, gain_two):
    breadth = level_ext.shape[3]
    xpad = jnp.pad(level_ext, ((0, 0), (0, 0), (0, 0), (1, 1)))
    stacked = jnp.concatenate(
        [xpad[..., 0:breadth], xpad[..., 1 : breadth + 1], xpad[..., 2 : breadth + 2]], axis=1
    )
    total = jnp.einsum(
        "oi,siyx->soyx", w_second[0], stacked[:, :, 0:count, :], preferred_element_type=jnp.float32
    )
    for tap_a in range(1, 3):
        total = total + jnp.einsum(
            "oi,siyx->soyx",
            w_second[tap_a],
            stacked[:, :, tap_a : tap_a + count, :],
            preferred_element_type=jnp.float32,
        )
    return normalize(total, gain_two).astype(jnp.bfloat16)


def column_conv(block, weight, rows_n, cols_n):
    depth = block.shape[0]
    zpad = jnp.pad(block, ((1, 1), (0, 0), (0, 0), (0, 0)))
    stacked = jnp.concatenate([zpad[0:depth], zpad[1 : depth + 1], zpad[2 : depth + 2]], axis=1)
    total = None
    for tap_b in range(3):
        for tap_e in range(3):
            term = jnp.einsum(
                "oi,siyx->soyx",
                weight[tap_b * 3 + tap_e],
                stacked[:, :, tap_b : tap_b + rows_n, tap_e : tap_e + cols_n],
                preferred_element_type=jnp.float32,
            )
            total = term if total is None else total + term
    return total


def pack_block(volume):
    depth, chans, rows_n, cols_n = volume.shape
    return volume.transpose(0, 2, 1, 3).reshape(1, depth, rows_n, chans * cols_n)


def cut_frames(planes, margin, block_w, blocks_n):
    padded = jnp.pad(planes, ((0, 0), (0, 0), (0, 0), (margin, margin)))
    frame_idx = (
        np.arange(blocks_n)[:, None] * block_w + np.arange(block_w + 2 * margin)[None, :]
    ).reshape(-1)
    return jnp.take(padded, jnp.asarray(frame_idx, jnp.int32), axis=3)


def shards(raw_image, w_first, gain_one, w_second, gain_two, offsets, w_third, w_fourth):
    local_secs = raw_image.shape[0]
    half_rows = raw_image.shape[1] // 2
    breadth = raw_image.shape[2] // 2
    blocks_n = lax.axis_size("sec")
    block_w = breadth // blocks_n
    sec_id = lax.axis_index("sec")
    upper_row = from_behind(raw_image[:, -1:, :], "strip", 1)
    rows_pad = jnp.concatenate([upper_row, raw_image], axis=1)
    level = first_level(rows_pad, half_rows, w_first, gain_one)
    level_ext = with_halo(level, (("strip", 2),), 1)
    feature = second_level(level_ext, half_rows, w_second, gain_two)
    row_ext = with_halo(feature, (("strip", 2),), OFF)
    own_offsets = lax.dynamic_slice_in_dim(offsets, sec_id * local_secs, local_secs, 0)

    def row_place(plane, shift):
        return lax.dynamic_slice_in_dim(plane, OFF + shift[0], half_rows, 1)

    row_shifted = jax.vmap(row_place)(row_ext, own_offsets)
    framed = cut_frames(row_shifted, OFF, block_w, blocks_n)
    received = lax.all_to_all(framed, "sec", split_axis=3, concat_axis=0, tiled=True)

    def col_place(plane, shift):
        return lax.dynamic_slice_in_dim(plane, OFF + shift[1], block_w, 2)

    aligned = jax.vmap(col_place)(received, offsets)
    rim_one = with_halo(aligned, (("sec", 3), ("strip", 2)), 1)
    middle = jax.nn.silu(column_conv(rim_one, w_third, half_rows, block_w)).astype(jnp.bfloat16)
    rim_two = with_halo(middle, (("sec", 3), ("strip", 2)), 1)
    return pack_block(column_conv(rim_two, w_fourth, half_rows, block_w))


def solution(mesh):
    placed = (P("sec", "strip", None), P(), P(), P(), P(), P(), P(), P())
    return jax.shard_map(
        shards, mesh=mesh, in_specs=placed, out_specs=P("sec", None, "strip", None), check_vma=False
    )
```

profile of v0, /device:TPU:27, one launch (start us, length us, event | category | flops | bytes accessed | tf_op | source)
XLA Modules:
  0.0 148.8 jit_solution(16678011316756802539)
XLA Ops:
  0.7 5.0 %collective-permute-start = (bf16[1,1,512]{2,1,0:T(2,128)(2,1)S(1)}, bf16[1,1,512]{2,1,0:T(2,128)(2,1)S(1)}, u32[]{:S(2)}, u32[]{:S(2)}) collective-permute-start(bf16[1,1,512]{2,1,0:T(2,128)(2,1)S(1)} %slice.219), channel_id=1, source_target_pairs={{0,1},{1,2},{2,3},{3,4},{4,5},{5,6},{6,7},{7,8},{8,9},{9,10},{10,1... | collective-permute-start | bytes 3080 | tf_op jit(solution)/shard_map/ppermute | solution.py:13
  11.5 5.4 %collective-permute-start.1 = (bf16[1,32,1,256]{3,1,2,0:T(8,128)(2,1)S(1)}, bf16[1,32,1,256]{3,1,2,0:T(8,128)(2,1)S(1)}, u32[]{:S(2)}, u32[]{:S(2)}) collective-permute-start(bf16[1,32,1,256]{3,1,2,0:T(8,128)(2,1)S(1)} %get-tuple-element.32), channel_id=1, source_target_pairs={{0,1},{1,2},{2,3},{3,4},{4,5},{5,6},{6,7},{7,8},{8,9},{9,10},{10,1... | collective-permute-start | bytes 49160 | tf_op jit(solution)/shard_map/ppermute | solution.py:21
  16.9 1.9 %collective-permute-start.2 = (bf16[1,32,1,256]{3,1,2,0:T(8,128)(2,1)S(1)}, bf16[1,32,1,256]{3,1,2,0:T(8,128)(2,1)S(1)}, u32[]{:S(2)}, u32[]{:S(2)}) collective-permute-start(bf16[1,32,1,256]{3,1,2,0:T(8,128)(2,1)S(1)} %get-tuple-element.33), channel_id=1, source_target_pairs={{1,0},{2,1},{3,2},{4,3},{5,4},{6,5},{7,6},{8,7},{9,8},{10,9},{11,1... | collective-permute-start | bytes 49160 | tf_op jit(solution)/shard_map/ppermute | solution.py:24
  18.8 4.3 %collective-permute-done.2 = bf16[1,32,1,256]{3,1,2,0:T(8,128)(2,1)S(1)} collective-permute-done((bf16[1,32,1,256]{3,1,2,0:T(8,128)(2,1)S(1)}, bf16[1,32,1,256]{3,1,2,0:T(8,128)(2,1)S(1)}, u32[]{:S(2)}, u32[]{:S(2)}) %collective-permute-start.2) | collective-permute-done | bytes 16416 | tf_op jit(solution)/shard_map/ppermute | solution.py:24
  26.9 4.9 %collective-permute-start.3 = (bf16[1,32,8,256]{3,1,2,0:T(8,128)(2,1)S(1)}, bf16[1,32,8,256]{3,1,2,0:T(8,128)(2,1)S(1)}, u32[]{:S(2)}, u32[]{:S(2)}) collective-permute-start(bf16[1,32,8,256]{3,1,2,0:T(8,128)(2,1)S(1)} %get-tuple-element.31), channel_id=1, source_target_pairs={{0,1},{1,2},{2,3},{3,4},{4,5},{5,6},{6,7},{7,8},{8,9},{9,10},{10,1... | collective-permute-start | bytes 393224 | tf_op jit(solution)/shard_map/ppermute | solution.py:21
  35.1 3.5 %gather_fusion = bf16[768,32,16]{1,2,0:T(8,128)(2,1)} fusion(bf16[32,16,272]{0,1,2:T(8,128)(2,1)S(1)} %copy.176, s32[1024]{0:T(1024)S(1)} %pad_clamp_fusion), kind=kCustom, calls=%fused_computation | custom fusion | bytes 1575936 | tf_op jit(solution)/shard_map/jit(_take)/gather | solution.py:95
  38.7 2.4 %bitcast_bitcast_fusion = bf16[768,1,16,32]{3,2,1,0:T(8,128)(2,1)S(1)} fusion(bf16[768,32,16]{1,2,0:T(8,128)(2,1)} %gather_fusion), kind=kLoop, calls=%fused_computation.143 | loop fusion | bytes 1572864
  41.1 3.8 %reshape.142 = bf16[32,2,6144]{2,1,0:T(2,128)(2,1)} reshape(bf16[768,1,16,32]{3,2,1,0:T(8,128)(2,1)S(1)} %bitcast_bitcast_fusion) | data formatting | bytes 1572864
  44.9 13.0 %all-to-all-start = ((bf16[32,2,6144]{2,1,0:T(2,128)(2,1)}), bf16[32,2,6144]{2,1,0:T(2,128)(2,1)}, u32[]{:S(2)}, u32[]{:S(2)}) async-start(bf16[32,2,6144]{2,1,0:T(2,128)(2,1)} %reshape.142), calls=%async_computation | async-start | bytes 1572864 | tf_op jit(solution)/shard_map/all_to_all | solution.py:118
  57.9 19.5 %all-to-all-done = bf16[32,2,6144]{2,1,0:T(2,128)(2,1)} async-done(((bf16[32,2,6144]{2,1,0:T(2,128)(2,1)}), bf16[32,2,6144]{2,1,0:T(2,128)(2,1)}, u32[]{:S(2)}, u32[]{:S(2)}) %all-to-all-start) | async-done | bytes 786464 | tf_op jit(solution)/shard_map/all_to_all | solution.py:118
  77.4 4.0 %reshape.143 = bf16[768,1,16,32]{3,2,1,0:T(8,128)(2,1)S(1)} reshape(bf16[32,2,6144]{2,1,0:T(2,128)(2,1)} %all-to-all-done) | data formatting | bytes 1572864
  81.4 2.5 %copy.209 = bf16[1,32,16,32,24]{1,2,3,4,0:T(8,128)(2,1)} copy(bf16[1,32,16,32,24]{1,2,4,3,0:T(8,128)(2,1)S(1)} %bitcast.241) | data formatting | bytes 1572864 | tf_op jit(solution)/shard_map/all_to_all | solution.py:118
  83.8 2.7 %gather_fusion.1 = bf16[32,32,16,8]{1,2,3,0:T(8,128)(2,1)S(1)} fusion(bf16[32,32,16,24]{1,2,0,3:T(8,128)(2,1)} %bitcast.240, s32[32]{0:T(128)S(1)} %or_bitcast_fusion), kind=kCustom, calls=%fused_computation.1 | custom fusion | bytes 524800 | tf_op jit(solution)/shard_map/vmap()/gather | solution.py:121
  86.6 4.8 %collective-permute-start.5 = (bf16[32,32,16,1]{1,0,3,2:T(8,128)(2,1)S(1)}, bf16[32,32,16,1]{1,0,3,2:T(8,128)(2,1)S(1)}, u32[]{:S(2)}, u32[]{:S(2)}) collective-permute-start(bf16[32,32,16,1]{1,0,3,2:T(8,128)(2,1)S(1)} %copy.207), channel_id=1, source_target_pairs={{0,16},{16,32},{32,48},{48,64},{64,80},{80,96},{96,112},{112,128},... | collective-permute-start | bytes 98312 | tf_op jit(solution)/shard_map/ppermute | solution.py:21
  91.5 2.8 %collective-permute-start.6 = (bf16[32,32,16,1]{1,0,3,2:T(8,128)(2,1)S(1)}, bf16[32,32,16,1]{1,0,3,2:T(8,128)(2,1)S(1)}, u32[]{:S(2)}, u32[]{:S(2)}) collective-permute-start(bf16[32,32,16,1]{1,0,3,2:T(8,128)(2,1)S(1)} %copy.208), channel_id=1, source_target_pairs={{16,0},{32,16},{48,32},{64,48},{80,64},{96,80},{112,96},{128,112},... | collective-permute-start | bytes 98312 | tf_op jit(solution)/shard_map/ppermute | solution.py:24
  95.2 2.3 %collective-permute-done.6 = bf16[32,32,16,1]{1,0,3,2:T(8,128)(2,1)S(1)} collective-permute-done((bf16[32,32,16,1]{1,0,3,2:T(8,128)(2,1)S(1)}, bf16[32,32,16,1]{1,0,3,2:T(8,128)(2,1)S(1)}, u32[]{:S(2)}, u32[]{:S(2)}) %collective-permute-start.6) | collective-permute-done | bytes 32800 | tf_op jit(solution)/shard_map/ppermute | solution.py:24
  97.6 4.2 %collective-permute-start.7 = (bf16[32,32,1,10]{1,0,3,2:T(8,128)(2,1)S(1)}, bf16[32,32,1,10]{1,0,3,2:T(8,128)(2,1)S(1)}, u32[]{:S(2)}, u32[]{:S(2)}) collective-permute-start(bf16[32,32,1,10]{1,0,3,2:T(8,128)(2,1)S(1)} %get-tuple-element.22), channel_id=1, source_target_pairs={{0,1},{1,2},{2,3},{3,4},{4,5},{5,6},{6,7},{7,8},{8,9},{9,10},{10,1... | collective-permute-start | bytes 61448 | tf_op jit(solution)/shard_map/ppermute | solution.py:21
  103.7 5.0 %collective-permute-done.8 = bf16[32,32,1,10]{1,0,3,2:T(8,128)(2,1)S(1)} collective-permute-done((bf16[32,32,1,10]{1,0,3,2:T(8,128)(2,1)S(1)}, bf16[32,32,1,10]{1,0,3,2:T(8,128)(2,1)S(1)}, u32[]{:S(2)}, u32[]{:S(2)}) %collective-permute-start.8) | collective-permute-done | bytes 20512 | tf_op jit(solution)/shard_map/ppermute | solution.py:24
  118.2 5.5 %collective-permute-start.10 = (bf16[32,32,16,1]{1,0,3,2:T(8,128)(2,1)S(1)}, bf16[32,32,16,1]{1,0,3,2:T(8,128)(2,1)S(1)}, u32[]{:S(2)}, u32[]{:S(2)}) collective-permute-start(bf16[32,32,16,1]{1,0,3,2:T(8,128)(2,1)S(1)} %get-tuple-element.25), channel_id=1, source_target_pairs={{16,0},{32,16},{48,32},{64,48},{80,64},{96,80},{112,96},{128,112},... | collective-permute-start | bytes 98312 | tf_op jit(solution)/shard_map/ppermute | solution.py:24
  125.7 3.0 %collective-permute-start.11 = (bf16[32,32,1,10]{1,0,3,2:T(8,128)(2,1)S(1)}, bf16[32,32,1,10]{1,0,3,2:T(8,128)(2,1)S(1)}, u32[]{:S(2)}, u32[]{:S(2)}) collective-permute-start(bf16[32,32,1,10]{1,0,3,2:T(8,128)(2,1)S(1)} %get-tuple-element.20), channel_id=1, source_target_pairs={{0,1},{1,2},{2,3},{3,4},{4,5},{5,6},{6,7},{7,8},{8,9},{9,10},{10,1... | collective-permute-start | bytes 61448 | tf_op jit(solution)/shard_map/ppermute | solution.py:21
  128.6 2.1 %collective-permute-start.12 = (bf16[32,32,1,10]{1,0,3,2:T(8,128)(2,1)S(1)}, bf16[32,32,1,10]{1,0,3,2:T(8,128)(2,1)S(1)}, u32[]{:S(2)}, u32[]{:S(2)}) collective-permute-start(bf16[32,32,1,10]{1,0,3,2:T(8,128)(2,1)S(1)} %get-tuple-element.21), channel_id=1, source_target_pairs={{1,0},{2,1},{3,2},{4,3},{5,4},{6,5},{7,6},{8,7},{9,8},{10,9},{11,1... | collective-permute-start | bytes 61448 | tf_op jit(solution)/shard_map/ppermute | solution.py:24
  130.8 4.8 %collective-permute-done.12 = bf16[32,32,1,10]{1,0,3,2:T(8,128)(2,1)S(1)} collective-permute-done((bf16[32,32,1,10]{1,0,3,2:T(8,128)(2,1)S(1)}, bf16[32,32,1,10]{1,0,3,2:T(8,128)(2,1)S(1)}, u32[]{:S(2)}, u32[]{:S(2)}) %collective-permute-start.12) | collective-permute-done | bytes 20512 | tf_op jit(solution)/shard_map/ppermute | solution.py:24
  143.1 2.3 %add_bitcast_fusion = f32[32,16,32,8]{2,0,3,1:T(8,128)} fusion(f32[32,16,8,32]{3,0,2,1:T(8,128)S(1)} %fusion.31, f32[32,16,8,32]{3,0,2,1:T(8,128)S(1)} %fusion.33, f32[32,16,8,32]{3,0,2,1:T(8,128)S(1)} %fusion.35, f32[32,16,8,32]{3,0,2,1:T(8,128)S(1)} %fusion.37, f32[32,16,8,32]{3,0,2,1:T(8,128)S(1)} %fusion.39, f32[32,16,8,32]{3,0,2,1:T(8,128)S(1)} %fusion.41, ...), kind=kOutput, calls=%fused_computation.11 | convolution fusion | flops 26214400 | bytes 18784256 | tf_op jit(solution)/shard_map/oi,siyx->soyx/dot_general | solution.py:75
  145.3 2.0 %copy.183 = f32[32,16,32,8]{0,3,2,1:T(8,128)S(1)} copy(f32[32,16,32,8]{2,0,3,1:T(8,128)} %add_bitcast_fusion) | data formatting | bytes 1048576 | tf_op jit(solution)/shard_map/add | solution.py:81
  (104 shorter events, 35.2 us)
Async XLA Ops:
  0.0 10.9 %copy-start = (bf16[9,32]{1,0:T(8,128)(2,1)S(1)}, bf16[9,32]{1,0:T(8,128)(2,1)}, u32[]{:S(2)}) copy-start(bf16[9,32]{1,0:T(8,128)(2,1)} %param.10) | copy-start | bytes 1732
  0.0 11.3 %copy-start.7 = (f32[32]{0:T(128)S(1)}, f32[32]{0:T(128)}, u32[]{:S(2)}) copy-start(f32[32]{0:T(128)} %param.11) | copy-start | bytes 388
  0.7 5.7 %collective-permute-start = (bf16[1,1,512]{2,1,0:T(2,128)(2,1)S(1)}, bf16[1,1,512]{2,1,0:T(2,128)(2,1)S(1)}, u32[]{:S(2)}, u32[]{:S(2)}) collective-permute-start(bf16[1,1,512]{2,1,0:T(2,128)(2,1)S(1)} %slice.219), channel_id=1, source_target_pairs={{0,1},{1,2},{2,3},{3,4},{4,5},{5,6},{6,7},{7,8},{8,9},{9,10},{10,1... | collective-permute-start | bytes 3080 | tf_op jit(solution)/shard_map/ppermute | solution.py:13
  11.5 7.3 %collective-permute-start.1 = (bf16[1,32,1,256]{3,1,2,0:T(8,128)(2,1)S(1)}, bf16[1,32,1,256]{3,1,2,0:T(8,128)(2,1)S(1)}, u32[]{:S(2)}, u32[]{:S(2)}) collective-permute-start(bf16[1,32,1,256]{3,1,2,0:T(8,128)(2,1)S(1)} %get-tuple-element.32), channel_id=1, source_target_pairs={{0,1},{1,2},{2,3},{3,4},{4,5},{5,6},{6,7},{7,8},{8,9},{9,10},{10,1... | collective-permute-start | bytes 49160 | tf_op jit(solution)/shard_map/ppermute | solution.py:21
  16.9 6.3 %collective-permute-start.2 = (bf16[1,32,1,256]{3,1,2,0:T(8,128)(2,1)S(1)}, bf16[1,32,1,256]{3,1,2,0:T(8,128)(2,1)S(1)}, u32[]{:S(2)}, u32[]{:S(2)}) collective-permute-start(bf16[1,32,1,256]{3,1,2,0:T(8,128)(2,1)S(1)} %get-tuple-element.33), channel_id=1, source_target_pairs={{1,0},{2,1},{3,2},{4,3},{5,4},{6,5},{7,6},{8,7},{9,8},{10,9},{11,1... | collective-permute-start | bytes 49160 | tf_op jit(solution)/shard_map/ppermute | solution.py:24
  18.8 4.8 %copy-start.4 = (bf16[3,32,96]{2,1,0:T(8,128)(2,1)S(1)}, bf16[3,32,96]{2,1,0:T(8,128)(2,1)}, u32[]{:S(2)}) copy-start(bf16[3,32,96]{2,1,0:T(8,128)(2,1)} %param.12) | copy-start | bytes 55300
  24.1 0.7 copy-start.8
  24.1 7.6 %copy-start.6 = (s32[32,2]{0,1:T(2,128)S(1)}, s32[32,2]{0,1:T(2,128)}, u32[]{:S(2)}) copy-start(s32[32,2]{0,1:T(2,128)} %param.14) | copy-start | bytes 772
  24.2 9.5 %copy-start.5 = (s32[768]{0:T(1024)S(1)}, s32[768]{0:T(1024)}, u32[]{:S(2)}) copy-start(s32[768]{0:T(1024)} %constant.127) | copy-start | bytes 9220
  24.9 8.7 %collective-permute-start.4 = (bf16[1,32,8,256]{3,1,2,0:T(8,128)(2,1)S(1)}, bf16[1,32,8,256]{3,1,2,0:T(8,128)(2,1)S(1)}, u32[]{:S(2)}, u32[]{:S(2)}) collective-permute-start(bf16[1,32,8,256]{3,1,2,0:T(8,128)(2,1)S(1)} %get-tuple-element.30), channel_id=1, source_target_pairs={{1,0},{2,1},{3,2},{4,3},{5,4},{6,5},{7,6},{8,7},{9,8},{10,9},{11,1... | collective-permute-start | bytes 393224 | tf_op jit(solution)/shard_map/ppermute | solution.py:24
  26.9 6.8 %collective-permute-start.3 = (bf16[1,32,8,256]{3,1,2,0:T(8,128)(2,1)S(1)}, bf16[1,32,8,256]{3,1,2,0:T(8,128)(2,1)S(1)}, u32[]{:S(2)}, u32[]{:S(2)}) collective-permute-start(bf16[1,32,8,256]{3,1,2,0:T(8,128)(2,1)S(1)} %get-tuple-element.31), channel_id=1, source_target_pairs={{0,1},{1,2},{2,3},{3,4},{4,5},{5,6},{6,7},{7,8},{8,9},{9,10},{10,1... | collective-permute-start | bytes 393224 | tf_op jit(solution)/shard_map/ppermute | solution.py:21
  44.9 32.5 %all-to-all-start = ((bf16[32,2,6144]{2,1,0:T(2,128)(2,1)}), bf16[32,2,6144]{2,1,0:T(2,128)(2,1)}, u32[]{:S(2)}, u32[]{:S(2)}) async-start(bf16[32,2,6144]{2,1,0:T(2,128)(2,1)} %reshape.142), calls=%async_computation | async-start | bytes 1572864 | tf_op jit(solution)/shard_map/all_to_all | solution.py:118
  86.6 7.8 %collective-permute-start.5 = (bf16[32,32,16,1]{1,0,3,2:T(8,128)(2,1)S(1)}, bf16[32,32,16,1]{1,0,3,2:T(8,128)(2,1)S(1)}, u32[]{:S(2)}, u32[]{:S(2)}) collective-permute-start(bf16[32,32,16,1]{1,0,3,2:T(8,128)(2,1)S(1)} %copy.207), channel_id=1, source_target_pairs={{0,16},{16,32},{32,48},{48,64},{64,80},{80,96},{96,112},{112,128},... | collective-permute-start | bytes 98312 | tf_op jit(solution)/shard_map/ppermute | solution.py:21
  91.5 6.1 %collective-permute-start.6 = (bf16[32,32,16,1]{1,0,3,2:T(8,128)(2,1)S(1)}, bf16[32,32,16,1]{1,0,3,2:T(8,128)(2,1)S(1)}, u32[]{:S(2)}, u32[]{:S(2)}) collective-permute-start(bf16[32,32,16,1]{1,0,3,2:T(8,128)(2,1)S(1)} %copy.208), channel_id=1, source_target_pairs={{16,0},{32,16},{48,32},{64,48},{80,64},{96,80},{112,96},{128,112},... | collective-permute-start | bytes 98312 | tf_op jit(solution)/shard_map/ppermute | solution.py:24
  97.6 6.1 %collective-permute-start.7 = (bf16[32,32,1,10]{1,0,3,2:T(8,128)(2,1)S(1)}, bf16[32,32,1,10]{1,0,3,2:T(8,128)(2,1)S(1)}, u32[]{:S(2)}, u32[]{:S(2)}) collective-permute-start(bf16[32,32,1,10]{1,0,3,2:T(8,128)(2,1)S(1)} %get-tuple-element.22), channel_id=1, source_target_pairs={{0,1},{1,2},{2,3},{3,4},{4,5},{5,6},{6,7},{7,8},{8,9},{9,10},{10,1... | collective-permute-start | bytes 61448 | tf_op jit(solution)/shard_map/ppermute | solution.py:21
  101.8 7.0 %collective-permute-start.8 = (bf16[32,32,1,10]{1,0,3,2:T(8,128)(2,1)S(1)}, bf16[32,32,1,10]{1,0,3,2:T(8,128)(2,1)S(1)}, u32[]{:S(2)}, u32[]{:S(2)}) collective-permute-start(bf16[32,32,1,10]{1,0,3,2:T(8,128)(2,1)S(1)} %get-tuple-element.23), channel_id=1, source_target_pairs={{1,0},{2,1},{3,2},{4,3},{5,4},{6,5},{7,6},{8,7},{9,8},{10,9},{11,1... | collective-permute-start | bytes 61448 | tf_op jit(solution)/shard_map/ppermute | solution.py:24
  110.4 1.4 copy-start.2
  116.3 7.8 %collective-permute-start.9 = (bf16[32,32,16,1]{1,0,3,2:T(8,128)(2,1)S(1)}, bf16[32,32,16,1]{1,0,3,2:T(8,128)(2,1)S(1)}, u32[]{:S(2)}, u32[]{:S(2)}) collective-permute-start(bf16[32,32,16,1]{1,0,3,2:T(8,128)(2,1)S(1)} %get-tuple-element.24), channel_id=1, source_target_pairs={{0,16},{16,32},{32,48},{48,64},{64,80},{80,96},{96,112},{112,128},... | collective-permute-start | bytes 98312 | tf_op jit(solution)/shard_map/ppermute | solution.py:21
  118.2 7.4 %collective-permute-start.10 = (bf16[32,32,16,1]{1,0,3,2:T(8,128)(2,1)S(1)}, bf16[32,32,16,1]{1,0,3,2:T(8,128)(2,1)S(1)}, u32[]{:S(2)}, u32[]{:S(2)}) collective-permute-start(bf16[32,32,16,1]{1,0,3,2:T(8,128)(2,1)S(1)} %get-tuple-element.25), channel_id=1, source_target_pairs={{16,0},{32,16},{48,32},{64,48},{80,64},{96,80},{112,96},{128,112},... | collective-permute-start | bytes 98312 | tf_op jit(solution)/shard_map/ppermute | solution.py:24
  125.7 5.1 %collective-permute-start.11 = (bf16[32,32,1,10]{1,0,3,2:T(8,128)(2,1)S(1)}, bf16[32,32,1,10]{1,0,3,2:T(8,128)(2,1)S(1)}, u32[]{:S(2)}, u32[]{:S(2)}) collective-permute-start(bf16[32,32,1,10]{1,0,3,2:T(8,128)(2,1)S(1)} %get-tuple-element.20), channel_id=1, source_target_pairs={{0,1},{1,2},{2,3},{3,4},{4,5},{5,6},{6,7},{7,8},{8,9},{9,10},{10,1... | collective-permute-start | bytes 61448 | tf_op jit(solution)/shard_map/ppermute | solution.py:21
  128.6 7.0 %collective-permute-start.12 = (bf16[32,32,1,10]{1,0,3,2:T(8,128)(2,1)S(1)}, bf16[32,32,1,10]{1,0,3,2:T(8,128)(2,1)S(1)}, u32[]{:S(2)}, u32[]{:S(2)}) collective-permute-start(bf16[32,32,1,10]{1,0,3,2:T(8,128)(2,1)S(1)} %get-tuple-element.21), channel_id=1, source_target_pairs={{1,0},{2,1},{3,2},{4,3},{5,4},{6,5},{7,6},{8,7},{9,8},{10,9},{11,1... | collective-permute-start | bytes 61448 | tf_op jit(solution)/shard_map/ppermute | solution.py:24
  138.3 1.4 copy-start.3
  145.3 3.5 %copy-start.1 = (bf16[9,32]{1,0:T(8,128)(2,1)S(1)}, bf16[9,32]{1,0:T(8,128)(2,1)}, u32[]{:S(2)}) copy-start(bf16[9,32]{1,0:T(8,128)(2,1)} %param.10) | copy-start | bytes 1732
where the time goes:
time: 150 us; the launch traced here: 149 us
  starting transfers between devices  58.2 us (39%)
  waiting for transfers between devices  38.8 us (26%)
  local copies, waits for them, and re-layouts  31.6 us (21%)
  matrix products  11.2 us (7%)
  other arithmetic  6.99 us (5%)
  between operations  2.04 us (1%)
    ppermute x6, starting transfers between devices, with_halo(): lax.ppermute(lax.slice_in_dim(block, block.shape[dim] - width, None, axis...  24.1 us
    all_to_all x1, waiting for transfers between devices, shards(): lax.all_to_all(framed, 'sec', split_axis=3, concat_axis=0, tiled=True)  19.5 us
    ppermute x6, waiting for transfers between devices, with_halo(): lax.ppermute(lax.slice_in_dim(block, 0, width, axis=dim), axis, backward)  18 us
    ppermute x6, starting transfers between devices, with_halo(): lax.ppermute(lax.slice_in_dim(block, 0, width, axis=dim), axis, backward)  16.1 us
    all_to_all x1, starting transfers between devices, shards(): lax.all_to_all(framed, 'sec', split_axis=3, concat_axis=0, tiled=True)  13 us
    unnamed x25, local copies, waits for them, and re-layouts  11.3 us
    dot_general x18, matrix products, column_conv(): jnp.einsum('oi,siyx->soyx', weight[tap_b * 3 + tap_e], stacked[:, :, tap_...  9.99 us
    ppermute x1, starting transfers between devices, from_behind(): return lax.ppermute(x, axis, pairs)  4.96 us
  transfers between devices with their start and end apart: 14, of which 9 were waited for; matrix products, arithmetic and copies ran while one was open for 1% of the time, Pallas kernels for 0%

commit v1 on v0

v1 whole, which is shorter than its diff:
```python
import jax
import jax.numpy as jnp
from jax import lax
from jax.experimental import pallas as pl
from jax.experimental.pallas import tpu as pltpu
from jax.sharding import PartitionSpec as P

C = 32
SECS = 32
BLOCK = 8
ROWS = 16
EXTENT = 256
RAW = 512
STRIPS = 16

F32, BF16 = jnp.float32, jnp.bfloat16
MESH_ID = pl.DeviceIdType.MESH


def iota(shape, axis):
    return lax.broadcasted_iota(jnp.int32, shape, axis)


def dot_nn(a, b):
    return jnp.dot(a, b, preferred_element_type=F32)


def dot_nt(a, b):
    return lax.dot_general(a, b, (((1,), (1,)), ((), ())), preferred_element_type=F32)


def silu(u):
    half = 0.5 * u
    return half + half * jnp.tanh(half)


def widen(ref, small, rows, count):
    ref[0:rows, :] = jnp.zeros((rows, 128), F32)
    ref[0:rows, 0:count] = small.astype(F32)
    return ref[0:rows, :]


def build_first(w_first, tile, band_one):
    base = widen(tile, w_first[...], 9, C)
    base = base + pltpu.roll(base, 32, 1)
    base = base + pltpu.roll(base, 64, 1)
    taps = jnp.concatenate([base] * 4, axis=1)
    lane = iota((32, 512), 1)
    column = 6 * (lane // 256) + (lane % 256) // 32
    shift = iota((32, 512), 0) - 1 - 2 * column
    band_one[...] = jnp.zeros(band_one.shape, BF16)
    for a, start in ((0, 32), (1, 128), (2, 160)):
        block = jnp.zeros((32, 512), F32)
        for b in range(3):
            block = jnp.where(shift == b, taps[3 * a + b : 3 * a + b + 1, :], block)
        for half in range(2):
            band_one[half, start + 64 * half : start + 64 * half + 32, :] = block.astype(BF16)


def build_gain(gain, tile):
    base = widen(tile, gain[...], 1, C)
    base = base + pltpu.roll(base, 32, 1)
    return base + pltpu.roll(base, 64, 1)


def build_second(w_second, wide, band_two):
    wide[...] = jnp.zeros(wide.shape, F32)
    for a in range(3):
        wide[:, 0:96] = w_second[a].astype(F32)
        base = wide[:, 0:256]
        for x in range(6):
            block = pltpu.roll(base, 32 * x, 1).astype(BF16) if x else base.astype(BF16)
            band_two[0, 32 * x : 32 * x + 32, 256 * a : 256 * a + 256] = block
            band_two[1, 64 + 32 * x : 96 + 32 * x, 256 * a : 256 * a + 256] = block
        band_two[0, 192:256, 256 * a : 256 * a + 256] = jnp.zeros((64, 256), BF16)
        band_two[1, 0:64, 256 * a : 256 * a + 256] = jnp.zeros((64, 256), BF16)


def tap_base(weight, wide, a, b):
    lane = iota((C, 128), 1)
    total = jnp.zeros((C, 128), F32)
    for e in range(3):
        wide[:, 0:96] = weight[3 * b + e].astype(F32)
        part = wide[:, 0:128]
        turn = (32 * (e - a)) % 128
        part = pltpu.roll(part, turn, 1) if turn else part
        total = jnp.where(lane // 32 == e, part, total)
    return jnp.concatenate([total, jnp.zeros((C, 256), F32)], axis=1)


def build_third(w_third, wide, band_three):
    wide[...] = jnp.zeros(wide.shape, F32)
    for a in range(3):
        for b in range(3):
            base = tap_base(w_third, wide, a, b)[:, 0:256]
            where = 3 * b + a
            for x in range(6):
                block = pltpu.roll(base, 32 * x, 1).astype(BF16) if x else base.astype(BF16)
                band_three[where, 32 * x : 32 * x + 32, :] = block
                if x >= 4:
                    band_three[where, 64 + 32 * x : 96 + 32 * x, :] = block


def build_fourth(w_fourth, wide, band_four):
    wide[...] = jnp.zeros(wide.shape, F32)
    row = iota((256, 256), 0)
    order = jnp.where(iota((256, 256), 1) == (row % BLOCK) * C + row // BLOCK, 1.0, 0.0).astype(BF16)
    for b in range(3):
        edges = []
        for a in range(3):
            base = tap_base(w_fourth, wide, a, b)
            stack = [
                (pltpu.roll(base, 32 * x, 1) if x else base).astype(BF16) for x in range(BLOCK)
            ]
            band = dot_nn(order, jnp.concatenate(stack, axis=0))
            band_four[b, :, 256 * a : 256 * a + 256] = band[:, 0:256].astype(BF16)
            edges.append(band[:, 256:384])
        band_four[b, :, 768:896] = (edges[0] + pltpu.roll(edges[1], 64, 1)).astype(BF16)
        band_four[b, :, 896:1024] = edges[2].astype(BF16)


def pick_rows(strip, dy):
    m = iota((64, 96), 0)
    half, parity, q = m // 32, (m // 16) % 2, m % 16
    row = 2 * (dy - 4 + 11 * half + q) + parity
    inside = (row + 32 * strip >= 0) & (row + 32 * strip < RAW)
    return jnp.where(inside & (iota((64, 96), 1) - 32 == row), 1.0, 0.0).astype(BF16)


def cut_windows(rows, dx, send):
    padded = jnp.concatenate([rows, jnp.zeros((64, 128), F32)], axis=1)
    shifted = pltpu.roll(padded, lax.rem(648 - 2 * dx, 640), 1)
    lane = iota((16, 128), 1)
    low = (lane // 64) == 0
    even = (lane // 32) % 2 == 0
    for odd in range(2):
        view = pltpu.roll(shifted, 624, 1) if odd else shifted
        for tile in range(4):
            parts = [view[16 * p : 16 * p + 16, 128 * tile : 128 * tile + 128] for p in range(4)]
            for m1 in range(2):
                pair = []
                for h0 in range(2):
                    first, second = parts[h0], parts[2 + h0]
                    if m1 == 0:
                        pair.append(jnp.where(low, first, pltpu.roll(second, 64, 1)))
                    else:
                        pair.append(jnp.where(low, pltpu.roll(first, 64, 1), second))
                group = 4 * tile + 2 * m1
                here = jnp.where(even, pair[0], pltpu.roll(pair[1], 32, 1))
                then = jnp.where(even, pltpu.roll(pair[0], 96, 1), pair[1])
                send[2 * group + odd] = here.astype(BF16)
                send[2 * (group + 1) + odd] = then.astype(BF16)


def first_layer(recv, band_one, gain, offsets, strip, block, stage, lhs, big, square, mean, level):
    stage[...] = recv[...].reshape(SECS * 16, 128).astype(F32)
    for q in range(12):
        piece = stage[pl.ds(q, SECS, stride=16), :].astype(BF16)
        if q < 11:
            lhs[32 * q : 32 * q + 32, 0:128] = piece
        if q > 0:
            lhs[32 * q - 32 : 32 * q, 128:256] = piece
    dy, dx = offsets[:, 0:1], offsets[:, 1:2]
    lane = iota((SECS, 512), 1)
    column = 6 * (lane // 256) + (lane % 256) // 32
    scale = jnp.where(column + dx + (BLOCK * block - 3) < EXTENT, jnp.concatenate([gain] * 4, axis=1), 0.0)
    for half in range(2):
        big[352 * half : 352 * half + 352, :] = dot_nn(lhs[...], band_one[half])
    normalize(big, square, mean, 22, 512)

    def finish(i, _):
        at = pl.ds(pl.multiple_of(32 * i, 32), 32)
        y = big[at, :] * lax.rsqrt(1.0 + mean[at, :]) * scale
        y = jnp.where(dy + (ROWS * strip - 3 + i) < EXTENT, y, 0.0)
        level[at, :] = y.astype(BF16)
        return 0

    lax.fori_loop(0, 22, finish, 0)


def normalize(big, square, mean, count, lanes):
    def one(i, _):
        at = pl.ds(pl.multiple_of(32 * i, 32), 32)
        v = silu(big[at, 0:lanes])
        big[at, 0:lanes] = v
        square[at, 0:lanes] = (v * v).astype(BF16)
        return 0

    lax.fori_loop(0, count, one, 0)
    same = iota((128, 128), 0) // C == iota((128, 128), 1) // C
    spread = jnp.where(same, 1.0 / C, 0.0).astype(BF16)
    for g in range(lanes // 128):
        mean[0 : 32 * count, 128 * g : 128 * g + 128] = dot_nn(
            square[0 : 32 * count, 128 * g : 128 * g + 128], spread
        )


def shift_sections(y, wide_lanes):
    s = iota((SECS, wide_lanes), 0)
    before = jnp.where(s == 0, 0.0, pltpu.roll(y, 1, 0))
    after = jnp.where(s == SECS - 1, 0.0, pltpu.roll(y, SECS - 1, 0))
    return before, after


def second_layer(level, band_two, gain, offsets, strip, block, big, square, mean, columns):
    parts = []
    for g in range(2):
        lhs = jnp.concatenate(
            [level[32 * a : 32 * a + 640, 256 * g : 256 * g + 256] for a in range(3)], axis=1
        )
        parts.append(dot_nt(lhs, band_two[g]))
    big[0:640, 0:128] = parts[0][:, 0:128]
    big[0:640, 128:256] = parts[0][:, 128:256] + parts[1][:, 0:128]
    big[0:640, 256:384] = parts[1][:, 128:256]
    normalize(big, square, mean, 20, 384)
    dy, dx = offsets[:, 0:1], offsets[:, 1:2]
    placed = iota((SECS, 384), 1) // C + (BLOCK * block - 2)
    inside = (placed >= 0) & (placed < EXTENT) & (placed + dx >= 0) & (placed + dx < EXTENT)
    scale = jnp.where(inside, jnp.concatenate([gain] * 3, axis=1), 0.0)

    def finish(i, _):
        at = pl.ds(pl.multiple_of(32 * i, 32), 32)
        y = big[at, 0:384] * lax.rsqrt(1.0 + mean[at, 0:384]) * scale
        row = ROWS * strip - 2 + i
        y = jnp.where((dy + row >= 0) & (dy + row < EXTENT), y, 0.0)
        y = jnp.where((row >= 0) & (row < EXTENT), y, 0.0)
        before, after = shift_sections(y, 384)
        columns[at, 0:384] = before.astype(BF16)
        columns[at, 384:768] = y.astype(BF16)
        columns[at, 768:1152] = after.astype(BF16)
        return 0

    lax.fori_loop(0, 20, finish, 0)


def third_layer(columns, band_three, strip, block, big, middle):
    for g in range(2):
        total = None
        for b in range(3):
            for a in range(3):
                lhs = columns[32 * b : 32 * b + 576, 384 * a + 128 * g : 384 * a + 128 * g + 256]
                rhs = band_three[3 * b + a]
                term = dot_nt(lhs, rhs if g else rhs[0:128])
                total = term if total is None else total + term
        if g:
            big[0:576, 128:384] = total
        else:
            big[0:576, 0:128] = total
    lane = iota((SECS, 384), 1)
    column = jnp.where(lane < 320, lane, lane - 64) // C + (BLOCK * block - 1)
    inside = (column >= 0) & (column < EXTENT)
    low = iota((SECS, 128), 1) < 64

    def finish(i, _):
        at = pl.ds(pl.multiple_of(32 * i, 32), 32)
        row = ROWS * strip - 1 + i
        y = silu(big[at, 0:384])
        y = jnp.where(inside & (row >= 0) & (row < EXTENT), y, 0.0)
        before, after = shift_sections(y, 384)
        middle[at, 0:256] = before[:, 0:256].astype(BF16)
        middle[at, 256:512] = y[:, 0:256].astype(BF16)
        middle[at, 512:768] = after[:, 0:256].astype(BF16)
        middle[at, 768:896] = jnp.where(low, before[:, 256:384], y[:, 256:384]).astype(BF16)
        middle[at, 896:1024] = after[:, 256:384].astype(BF16)
        return 0

    lax.fori_loop(0, 18, finish, 0)


def fourth_layer(middle, band_four, big, out):
    total = None
    for b in range(3):
        term = dot_nt(middle[32 * b : 32 * b + 512, :], band_four[b])
        total = term if total is None else total + term
    big[0:512, 0:256] = total
    for i in range(ROWS):
        out[:, i, :] = big[32 * i : 32 * i + 32, 0:256]


def kernel(
    raw, w_first, gain_one, w_second, gain_two, offsets, offsets_smem, w_third, w_fourth, out,
    ext, send, recv, band_one, band_two, band_three, band_four, tile, wide, stage, lhs, big, square,
    mean, level, columns, middle, halo_send, halo_recv, pass_send, pass_recv,
):
    me, strip = lax.axis_index("sec"), lax.axis_index("strip")
    up = lax.rem(strip + STRIPS - 1, STRIPS)
    down = lax.rem(strip + 1, STRIPS)

    barrier = pltpu.get_barrier_semaphore()
    for near in (up, down):
        pl.semaphore_signal(barrier, inc=1, device_id={"strip": near}, device_id_type=MESH_ID)
    for d in range(1, SECS):
        peer = lax.rem(me + d, SECS)
        pl.semaphore_signal(barrier, inc=1, device_id={"sec": peer}, device_id_type=MESH_ID)

    ext[32:64, :] = raw[...]
    pl.semaphore_wait(barrier, SECS + 1)

    halos = []
    for n, (near, start) in enumerate(((down, 0), (up, 64))):
        copy = pltpu.make_async_remote_copy(
            src_ref=ext.at[32:64, :], dst_ref=ext.at[start : start + 32, :],
            send_sem=halo_send.at[n], recv_sem=halo_recv.at[n],
            device_id={"strip": near}, device_id_type=MESH_ID,
        )
        copy.start()
        halos.append(copy)
    build_first(w_first, tile, band_one)
    build_second(w_second, wide, band_two)
    dy, dx = offsets_smem[me, 0], offsets_smem[me, 1]
    chosen = pick_rows(strip, dy)
    for copy in halos:
        copy.wait()
    cut_windows(dot_nn(chosen, ext[...]), dx, send)

    for d in range(1, SECS):
        peer = lax.rem(me + d, SECS)
        pltpu.make_async_remote_copy(
            src_ref=send.at[peer], dst_ref=recv.at[me], send_sem=pass_send, recv_sem=pass_recv,
            device_id={"sec": peer}, device_id_type=MESH_ID,
        ).start()
    recv[me] = send[me]
    build_third(w_third, wide, band_three)
    build_fourth(w_fourth, wide, band_four)
    gain_a, gain_b = build_gain(gain_one, tile), build_gain(gain_two, tile)
    pltpu.make_async_copy(send.at[0 : SECS - 1], recv.at[0 : SECS - 1], pass_recv).wait()
    pltpu.make_async_copy(send.at[0 : SECS - 1], recv.at[0 : SECS - 1], pass_send).wait()

    first_layer(recv, band_one, gain_a, offsets, strip, me, stage, lhs, big, square, mean, level)
    second_layer(level, band_two, gain_b, offsets, strip, me, big, square, mean, columns)
    third_layer(columns, band_three, strip, me, big, middle)
    fourth_layer(middle, band_four, big, out)


def shards(raw_image, w_first, gain_one, w_second, gain_two, offsets, w_third, w_fourth):
    vmem = pl.BlockSpec(memory_space=pltpu.VMEM)
    smem = pl.BlockSpec(memory_space=pltpu.SMEM)
    result = pl.pallas_call(
        kernel,
        out_shape=jax.ShapeDtypeStruct((SECS, ROWS, C * BLOCK), F32),
        in_specs=[vmem] * 6 + [smem] + [vmem] * 2,
        out_specs=vmem,
        scratch_shapes=[
            pltpu.VMEM((96, RAW), BF16),
            pltpu.VMEM((SECS, 16, 128), BF16),
            pltpu.VMEM((SECS, 16, 128), BF16),
            pltpu.VMEM((2, 256, 512), BF16),
            pltpu.VMEM((2, 256, 768), BF16),
            pltpu.VMEM((9, 256, 256), BF16),
            pltpu.VMEM((3, 256, 1024), BF16),
            pltpu.VMEM((16, 128), F32),
            pltpu.VMEM((C, 256), F32),
            pltpu.VMEM((SECS * 16, 128), F32),
            pltpu.VMEM((352, 256), BF16),
            pltpu.VMEM((704, 512), F32),
            pltpu.VMEM((704, 512), BF16),
            pltpu.VMEM((704, 512), F32),
            pltpu.VMEM((704, 512), BF16),
            pltpu.VMEM((640, 1152), BF16),
            pltpu.VMEM((576, 1024), BF16),
            pltpu.SemaphoreType.DMA((2,)),
            pltpu.SemaphoreType.DMA((2,)),
            pltpu.SemaphoreType.DMA,
            pltpu.SemaphoreType.DMA,
        ],
        compiler_params=pltpu.CompilerParams(
            collective_id=0, has_side_effects=True, vmem_limit_bytes=48 * 2**20
        ),
        cost_estimate=pl.CostEstimate(flops=10**9, bytes_accessed=2**20, transcendentals=10**6),
    )(
        raw_image.reshape(32, RAW), w_first, gain_one.reshape(1, C), w_second,
        gain_two.reshape(1, C), offsets, offsets, w_third, w_fourth,
    )
    return result.reshape(1, SECS, ROWS, C * BLOCK)


def solution(mesh):
    placed = (P("sec", "strip", None), P(), P(), P(), P(), P(), P(), P())
    return jax.shard_map(
        shards, mesh=mesh, in_specs=placed, out_specs=P("sec", None, "strip", None), check_vma=False
    )
```

time: 150 us -> 40.6 us (0.27)
  the two profiles are of different devices: /device:TPU:27 before, /device:TPU:25 now
where the time goes in v1:
time: 40.6 us; the launch traced here: 40.2 us
  Pallas kernels  34.8 us (86%)
  local copies, waits for them, and re-layouts  5.43 us (13%)
    pallas_call x1, Pallas kernels, shards(): pl.pallas_call(kernel, out_shape=jax.ShapeDtypeStruct((SECS, ROWS, C * BL...  34.8 us
    unnamed x18, local copies, waits for them, and re-layouts  5.43 us

profile of v1, /device:TPU:25, one launch (start us, length us, event | category | flops | bytes accessed | tf_op | source)
XLA Modules:
  0.0 40.2 jit_solution(16542973230459578340)
XLA Ops:
  0.0 0.0 copy-start.7
  0.0 0.7 %copy-done.7 = s32[32,2]{0,1:T(2,128)S(1)} copy-done((s32[32,2]{0,1:T(2,128)S(1)}, s32[32,2]{0,1:T(2,128)}, u32[]{:S(2)}) %copy-start.7) | copy-done | bytes 280
  0.7 0.0 copy-start.4
  0.7 0.0 copy-start.5
  0.7 0.0 copy-start.6
  0.7 0.1 copy.9.offsets.offsets_smem
  0.8 0.6 %copy-done.4 = bf16[9,32]{1,0:T(8,128)(2,1)S(1)} copy-done((bf16[9,32]{1,0:T(8,128)(2,1)S(1)}, bf16[9,32]{1,0:T(8,128)(2,1)}, u32[]{:S(2)}) %copy-start.4) | copy-done | bytes 600
  1.4 0.0 copy-done.5
  1.4 0.0 copy-done.6
  1.4 0.0 copy-start
  1.4 0.9 %copy-done = bf16[9,32,96]{2,1,0:T(8,128)(2,1)S(1)} copy-done((bf16[9,32,96]{2,1,0:T(8,128)(2,1)S(1)}, bf16[9,32,96]{2,1,0:T(8,128)(2,1)}, u32[]{:S(2)}) %copy-start) | copy-done | bytes 55320
  2.3 0.0 copy-start.1
  2.3 0.9 %copy-done.1 = bf16[9,32,96]{2,1,0:T(8,128)(2,1)S(1)} copy-done((bf16[9,32,96]{2,1,0:T(8,128)(2,1)S(1)}, bf16[9,32,96]{2,1,0:T(8,128)(2,1)}, u32[]{:S(2)}) %copy-start.1) | copy-done | bytes 55320
  3.1 0.0 copy-start.2
  3.1 0.8 %copy-done.2 = bf16[1,32,512]{2,1,0:T(8,128)(2,1)S(1)} copy-done((bf16[1,32,512]{2,1,0:T(8,128)(2,1)S(1)}, bf16[1,32,512]{2,1,0:T(8,128)(2,1)}, u32[]{:S(2)}) %copy-start.2) | copy-done | bytes 32792
  3.9 0.0 copy-start.3
  3.9 0.7 %copy-done.3 = bf16[3,32,96]{2,1,0:T(8,128)(2,1)S(1)} copy-done((bf16[3,32,96]{2,1,0:T(8,128)(2,1)S(1)}, bf16[3,32,96]{2,1,0:T(8,128)(2,1)}, u32[]{:S(2)}) %copy-start.3) | copy-done | bytes 18456
  4.6 34.8 %shard_map.82 = f32[32,16,256]{2,1,0:T(8,128)S(1)} custom-call(bf16[32,512]{1,0:T(8,128)(2,1)S(1)} %bitcast.5, bf16[9,32]{1,0:T(8,128)(2,1)S(1)} %copy-done.4, f32[1,32]{1,0:T(1,128)S(1)} %bitcast.6, bf16[3,32,96]{2,1,0:T(8,128)(2,1)S(1)} %copy-done.3, f32[1,32]{1,0:T(1,128)S(1)} %bitcast.7, s32[32,2]{1,0:T(8,128)S(1)} %copy.9.offsets.offsets_smem, ...), custom_call_target="tpu_custom_call" | custom-call | flops 1000000000 | bytes 1048576 | tf_op jit(solution)/shard_map/pallas_call | solution.py:338
  39.4 0.8 %copy.12 = f32[1,32,16,256]{3,2,1,0:T(8,128)} copy(f32[1,32,16,256]{3,2,1,0:T(8,128)S(1)} %bitcast.4) | data formatting | bytes 1048576
Async XLA Ops:
  0.0 0.7 %copy-start.7 = (s32[32,2]{0,1:T(2,128)S(1)}, s32[32,2]{0,1:T(2,128)}, u32[]{:S(2)}) copy-start(s32[32,2]{0,1:T(2,128)} %param.13) | copy-start | bytes 772
  0.7 0.7 %copy-start.4 = (bf16[9,32]{1,0:T(8,128)(2,1)S(1)}, bf16[9,32]{1,0:T(8,128)(2,1)}, u32[]{:S(2)}) copy-start(bf16[9,32]{1,0:T(8,128)(2,1)} %w_first.1) | copy-start | bytes 1732
  0.7 0.7 %copy-start.5 = (f32[32]{0:T(128)S(1)}, f32[32]{0:T(128)}, u32[]{:S(2)}) copy-start(f32[32]{0:T(128)} %param.10) | copy-start | bytes 388
  0.7 0.7 %copy-start.6 = (f32[32]{0:T(128)S(1)}, f32[32]{0:T(128)}, u32[]{:S(2)}) copy-start(f32[32]{0:T(128)} %param.12) | copy-start | bytes 388
  1.4 0.9 %copy-start = (bf16[9,32,96]{2,1,0:T(8,128)(2,1)S(1)}, bf16[9,32,96]{2,1,0:T(8,128)(2,1)}, u32[]{:S(2)}) copy-start(bf16[9,32,96]{2,1,0:T(8,128)(2,1)} %w_third.1) | copy-start | bytes 165892
  2.3 0.9 %copy-start.1 = (bf16[9,32,96]{2,1,0:T(8,128)(2,1)S(1)}, bf16[9,32,96]{2,1,0:T(8,128)(2,1)}, u32[]{:S(2)}) copy-start(bf16[9,32,96]{2,1,0:T(8,128)(2,1)} %w_fourth.1) | copy-start | bytes 165892
  3.1 0.8 %copy-start.2 = (bf16[1,32,512]{2,1,0:T(8,128)(2,1)S(1)}, bf16[1,32,512]{2,1,0:T(8,128)(2,1)}, u32[]{:S(2)}) copy-start(bf16[1,32,512]{2,1,0:T(8,128)(2,1)} %param.8) | copy-start | bytes 98308
  3.9 0.7 %copy-start.3 = (bf16[3,32,96]{2,1,0:T(8,128)(2,1)S(1)}, bf16[3,32,96]{2,1,0:T(8,128)(2,1)}, u32[]{:S(2)}) copy-start(bf16[3,32,96]{2,1,0:T(8,128)(2,1)} %w_second.1) | copy-start | bytes 55300

commit v2 on v1

--- a/solution.py
+++ b/solution.py
@@ -15,6 +15,16 @@
 
 F32, BF16 = jnp.float32, jnp.bfloat16
 MESH_ID = pl.DeviceIdType.MESH
+
+
+PEERS = sorted(
+    [(x, z) for x in range(4) for z in range(8) if x or z],
+    key=lambda at: -(min(at[0], 4 - at[0]) + min(at[1], 8 - at[1])),
+)
+
+
+def peer_at(me, x, z):
+    return lax.rem(me // 8 + x, 4) * 8 + lax.rem(lax.rem(me, 8) + z, 8)
 
 
 def iota(shape, axis):
@@ -152,6 +162,11 @@
                 send[2 * (group + 1) + odd] = then.astype(BF16)
 
 
+def as_column(row):
+    same = iota((SECS, SECS), 0) == iota((SECS, SECS), 1)
+    return jnp.sum(jnp.where(same, row.astype(F32), 0.0), axis=1, keepdims=True).astype(jnp.int32)
+
+
 def first_layer(recv, band_one, gain, offsets, strip, block, stage, lhs, big, square, mean, level):
     stage[...] = recv[...].reshape(SECS * 16, 128).astype(F32)
     for q in range(12):
@@ -160,7 +175,7 @@
             lhs[32 * q : 32 * q + 32, 0:128] = piece
         if q > 0:
             lhs[32 * q - 32 : 32 * q, 128:256] = piece
-    dy, dx = offsets[:, 0:1], offsets[:, 1:2]
+    dy, dx = as_column(offsets[0:1, :]), as_column(offsets[1:2, :])
     lane = iota((SECS, 512), 1)
     column = 6 * (lane // 256) + (lane % 256) // 32
     scale = jnp.where(column + dx + (BLOCK * block - 3) < EXTENT, jnp.concatenate([gain] * 4, axis=1), 0.0)
@@ -175,7 +190,7 @@
         level[at, :] = y.astype(BF16)
         return 0
 
-    lax.fori_loop(0, 22, finish, 0)
+    lax.fori_loop(0, 22, finish, 0, unroll=True)
 
 
 def normalize(big, square, mean, count, lanes):
@@ -186,7 +201,7 @@
         square[at, 0:lanes] = (v * v).astype(BF16)
         return 0
 
-    lax.fori_loop(0, count, one, 0)
+    lax.fori_loop(0, count, one, 0, unroll=True)
     same = iota((128, 128), 0) // C == iota((128, 128), 1) // C
     spread = jnp.where(same, 1.0 / C, 0.0).astype(BF16)
     for g in range(lanes // 128):
@@ -213,7 +228,7 @@
     big[0:640, 128:256] = parts[0][:, 128:256] + parts[1][:, 0:128]
     big[0:640, 256:384] = parts[1][:, 128:256]
     normalize(big, square, mean, 20, 384)
-    dy, dx = offsets[:, 0:1], offsets[:, 1:2]
+    dy, dx = as_column(offsets[0:1, :]), as_column(offsets[1:2, :])
     placed = iota((SECS, 384), 1) // C + (BLOCK * block - 2)
     inside = (placed >= 0) & (placed < EXTENT) & (placed + dx >= 0) & (placed + dx < EXTENT)
     scale = jnp.where(inside, jnp.concatenate([gain] * 3, axis=1), 0.0)
@@ -230,7 +245,7 @@
         columns[at, 768:1152] = after.astype(BF16)
         return 0
 
-    lax.fori_loop(0, 20, finish, 0)
+    lax.fori_loop(0, 20, finish, 0, unroll=True)
 
 
 def third_layer(columns, band_three, strip, block, big, middle):
@@ -264,7 +279,7 @@
         middle[at, 896:1024] = after[:, 256:384].astype(BF16)
         return 0
 
-    lax.fori_loop(0, 18, finish, 0)
+    lax.fori_loop(0, 18, finish, 0, unroll=True)
 
 
 def fourth_layer(middle, band_four, big, out):
@@ -278,22 +293,44 @@
 
 
 def kernel(
-    raw, w_first, gain_one, w_second, gain_two, offsets, offsets_smem, w_third, w_fourth, out,
+    raw_hbm, w_first_hbm, gain_one_hbm, w_second_hbm, gain_two_hbm, offsets_hbm, w_third_hbm,
+    w_fourth_hbm, out,
+    w_first, gain_one, w_second, gain_two, offsets, w_third, w_fourth, offsets_smem,
     ext, send, recv, band_one, band_two, band_three, band_four, tile, wide, stage, lhs, big, square,
-    mean, level, columns, middle, halo_send, halo_recv, pass_send, pass_recv,
+    mean, level, columns, middle, load_sem, halo_send, halo_recv, pass_send, pass_recv,
 ):
     me, strip = lax.axis_index("sec"), lax.axis_index("strip")
     up = lax.rem(strip + STRIPS - 1, STRIPS)
     down = lax.rem(strip + 1, STRIPS)
 
+    loads = [
+        pltpu.make_async_copy(source, target, load_sem.at[n])
+        for n, (source, target) in enumerate(
+            (
+                (raw_hbm, ext.at[32:64, :]),
+                (offsets_hbm, offsets_smem),
+                (w_first_hbm, w_first),
+                (w_second_hbm, w_second),
+                (w_third_hbm, w_third),
+                (w_fourth_hbm, w_fourth),
+                (gain_one_hbm, gain_one),
+                (gain_two_hbm, gain_two),
+                (offsets_hbm, offsets),
+            )
+        )
+    ]
+    for load in loads:
+        load.start()
+
     barrier = pltpu.get_barrier_semaphore()
     for near in (up, down):
         pl.semaphore_signal(barrier, inc=1, device_id={"strip": near}, device_id_type=MESH_ID)
-    for d in range(1, SECS):
-        peer = lax.rem(me + d, SECS)
+    for x, z in PEERS:
+        peer = peer_at(me, x, z)
         pl.semaphore_signal(barrier, inc=1, device_id={"sec": peer}, device_id_type=MESH_ID)
 
-    ext[32:64, :] = raw[...]
+    for load in loads:
+        load.wait()
     pl.semaphore_wait(barrier, SECS + 1)
 
     halos = []
@@ -307,14 +344,14 @@
         halos.append(copy)
     build_first(w_first, tile, band_one)
     build_second(w_second, wide, band_two)
-    dy, dx = offsets_smem[me, 0], offsets_smem[me, 1]
+    dy, dx = offsets_smem[0, me], offsets_smem[1, me]
     chosen = pick_rows(strip, dy)
     for copy in halos:
-        copy.wait()
+        copy.wait_recv()
     cut_windows(dot_nn(chosen, ext[...]), dx, send)
 
-    for d in range(1, SECS):
-        peer = lax.rem(me + d, SECS)
+    for x, z in PEERS:
+        peer = peer_at(me, x, z)
         pltpu.make_async_remote_copy(
             src_ref=send.at[peer], dst_ref=recv.at[me], send_sem=pass_send, recv_sem=pass_recv,
             device_id={"sec": peer}, device_id_type=MESH_ID,
@@ -325,6 +362,8 @@
     gain_a, gain_b = build_gain(gain_one, tile), build_gain(gain_two, tile)
     pltpu.make_async_copy(send.at[0 : SECS - 1], recv.at[0 : SECS - 1], pass_recv).wait()
     pltpu.make_async_copy(send.at[0 : SECS - 1], recv.at[0 : SECS - 1], pass_send).wait()
+    for copy in halos:
+        copy.wait_send()
 
     first_layer(recv, band_one, gain_a, offsets, strip, me, stage, lhs, big, square, mean, level)
     second_layer(level, band_two, gain_b, offsets, strip, me, big, square, mean, columns)
@@ -333,14 +372,21 @@
 
 
 def shards(raw_image, w_first, gain_one, w_second, gain_two, offsets, w_third, w_fourth):
-    vmem = pl.BlockSpec(memory_space=pltpu.VMEM)
-    smem = pl.BlockSpec(memory_space=pltpu.SMEM)
+    hbm = pl.BlockSpec(memory_space=pltpu.HBM)
     result = pl.pallas_call(
         kernel,
         out_shape=jax.ShapeDtypeStruct((SECS, ROWS, C * BLOCK), F32),
-        in_specs=[vmem] * 6 + [smem] + [vmem] * 2,
-        out_specs=vmem,
+        in_specs=[hbm] * 8,
+        out_specs=pl.BlockSpec(memory_space=pltpu.VMEM),
         scratch_shapes=[
+            pltpu.VMEM((9, C), BF16),
+            pltpu.VMEM((1, C), F32),
+            pltpu.VMEM((3, C, 96), BF16),
+            pltpu.VMEM((1, C), F32),
+            pltpu.VMEM((2, SECS), jnp.int32),
+            pltpu.VMEM((9, C, 96), BF16),
+            pltpu.VMEM((9, C, 96), BF16),
+            pltpu.SMEM((2, SECS), jnp.int32),
             pltpu.VMEM((96, RAW), BF16),
             pltpu.VMEM((SECS, 16, 128), BF16),
             pltpu.VMEM((SECS, 16, 128), BF16),
@@ -358,18 +404,19 @@
             pltpu.VMEM((704, 512), BF16),
             pltpu.VMEM((640, 1152), BF16),
             pltpu.VMEM((576, 1024), BF16),
+            pltpu.SemaphoreType.DMA((9,)),
             pltpu.SemaphoreType.DMA((2,)),
             pltpu.SemaphoreType.DMA((2,)),
             pltpu.SemaphoreType.DMA,
             pltpu.SemaphoreType.DMA,
         ],
         compiler_params=pltpu.CompilerParams(
-            collective_id=0, has_side_effects=True, vmem_limit_bytes=48 * 2**20
+            collective_id=0, has_side_effects=True, vmem_limit_bytes=60 * 2**20
         ),
         cost_estimate=pl.CostEstimate(flops=10**9, bytes_accessed=2**20, transcendentals=10**6),
     )(
         raw_image.reshape(32, RAW), w_first, gain_one.reshape(1, C), w_second,
-        gain_two.reshape(1, C), offsets, offsets, w_third, w_fourth,
+        gain_two.reshape(1, C), offsets.T, w_third, w_fourth,
     )
     return result.reshape(1, SECS, ROWS, C * BLOCK)
 

time: 40.6 us -> 31.7 us (0.78)
  Pallas kernels: 34.8 us -> 29.6 us
  local copies, waits for them, and re-layouts: 5.43 us -> 1.87 us
    pallas_call x1, Pallas kernels: 34.8 us -> 29.6 us  [shards(): pl.pallas_call(kernel, out_shape=jax.ShapeDtypeStruct((SECS, ROWS, C * BL...]
    unnamed x18 -> x1, local copies, waits for them, and re-layouts: 5.43 us -> 1.87 us
where the time goes in v2:
time: 31.7 us; the launch traced here: 31.5 us
  Pallas kernels  29.6 us (93%)
  local copies, waits for them, and re-layouts  1.87 us (6%)
    pallas_call x1, Pallas kernels, shards(): pl.pallas_call(kernel, out_shape=jax.ShapeDtypeStruct((SECS, ROWS, C * BL...  29.6 us
    unnamed x1, local copies, waits for them, and re-layouts  1.87 us

profile of v2, /device:TPU:25, one launch (start us, length us, event | category | flops | bytes accessed | tf_op | source)
XLA Modules:
  0.0 31.5 jit_solution(7676272455197695187)
XLA Ops:
  0.0 29.6 %shard_map.82 = f32[32,16,256]{2,1,0:T(8,128)} custom-call(bf16[32,512]{1,0:T(8,128)(2,1)} %bitcast.6, bf16[9,32]{1,0:T(8,128)(2,1)} %w_first_hbm.1, f32[1,32]{1,0:T(1,128)} %bitcast.8, bf16[3,32,96]{2,1,0:T(8,128)(2,1)} %w_second_hbm.1, f32[1,32]{1,0:T(1,128)} %bitcast.9, s32[2,32]{1,0:T(2,128)} %bitcast.7, bf16[9,32,96]{2,1,0:T(8,128)(2,1)} %w_third_hbm.1, ...), custom_call_target="tpu_custom_call" | custom-call | flops 1000000000 | bytes 1048576 | tf_op jit(solution)/shard_map/pallas_call | solution.py:376
  29.7 1.9 %copy.10 = f32[1,32,16,256]{3,2,1,0:T(8,128)} copy(f32[1,32,16,256]{3,2,1,0:T(8,128)} %bitcast.5) | data formatting | bytes 1048576

commit v3 on v2

--- a/solution.py
+++ b/solution.py
@@ -167,7 +167,14 @@
     return jnp.sum(jnp.where(same, row.astype(F32), 0.0), axis=1, keepdims=True).astype(jnp.int32)
 
 
-def first_layer(recv, band_one, gain, offsets, strip, block, stage, lhs, big, square, mean, level):
+FIRST, SECOND, THIRD, FOURTH = (0, 11, 22), (0, 9, 20), (0, 9, 18), (0, 16)
+
+
+def span(start, stop):
+    return slice(32 * start, 32 * stop)
+
+
+def gather_first(recv, stage, lhs):
     stage[...] = recv[...].reshape(SECS * 16, 128).astype(F32)
     for q in range(12):
         piece = stage[pl.ds(q, SECS, stride=16), :].astype(BF16)
@@ -175,39 +182,20 @@
             lhs[32 * q : 32 * q + 32, 0:128] = piece
         if q > 0:
             lhs[32 * q - 32 : 32 * q, 128:256] = piece
-    dy, dx = as_column(offsets[0:1, :]), as_column(offsets[1:2, :])
-    lane = iota((SECS, 512), 1)
-    column = 6 * (lane // 256) + (lane % 256) // 32
-    scale = jnp.where(column + dx + (BLOCK * block - 3) < EXTENT, jnp.concatenate([gain] * 4, axis=1), 0.0)
-    for half in range(2):
-        big[352 * half : 352 * half + 352, :] = dot_nn(lhs[...], band_one[half])
-    normalize(big, square, mean, 22, 512)
-
-    def finish(i, _):
-        at = pl.ds(pl.multiple_of(32 * i, 32), 32)
-        y = big[at, :] * lax.rsqrt(1.0 + mean[at, :]) * scale
-        y = jnp.where(dy + (ROWS * strip - 3 + i) < EXTENT, y, 0.0)
-        level[at, :] = y.astype(BF16)
-        return 0
-
-    lax.fori_loop(0, 22, finish, 0, unroll=True)
-
-
-def normalize(big, square, mean, count, lanes):
-    def one(i, _):
-        at = pl.ds(pl.multiple_of(32 * i, 32), 32)
-        v = silu(big[at, 0:lanes])
-        big[at, 0:lanes] = v
-        square[at, 0:lanes] = (v * v).astype(BF16)
-        return 0
-
-    lax.fori_loop(0, count, one, 0, unroll=True)
-    same = iota((128, 128), 0) // C == iota((128, 128), 1) // C
+
+
+def normalize(big, square, start, stop, lanes):
+    for i in range(start, stop):
+        v = silu(big[span(i, i + 1), 0:lanes])
+        big[span(i, i + 1), 0:lanes] = v
+        square[span(i, i + 1), 0:lanes] = (v * v).astype(BF16)
+    same = iota((256, 256), 0) // C == iota((256, 256), 1) // C
     spread = jnp.where(same, 1.0 / C, 0.0).astype(BF16)
-    for g in range(lanes // 128):
-        mean[0 : 32 * count, 128 * g : 128 * g + 128] = dot_nn(
-            square[0 : 32 * count, 128 * g : 128 * g + 128], spread
-        )
+    parts = []
+    for low in range(0, lanes, 256):
+        wide = min(256, lanes - low)
+        parts.append(dot_nn(square[span(start, stop), low : low + wide], spread[0:wide, 0:wide]))
+    return jnp.concatenate(parts, axis=1)
 
 
 def shift_sections(y, wide_lanes):
@@ -217,87 +205,141 @@
     return before, after
 
 
-def second_layer(level, band_two, gain, offsets, strip, block, big, square, mean, columns):
+def first_multiply(half, lhs, band_one, big):
+    big[span(11 * half, 11 * half + 11), :] = dot_nn(lhs[...], band_one[half])
+
+
+def first_scale(gain, dx, block):
+    lane = iota((SECS, 512), 1)
+    column = 6 * (lane // 256) + (lane % 256) // 32
+    inside = column + dx + (BLOCK * block - 3) < EXTENT
+    return jnp.where(inside, jnp.concatenate([gain] * 4, axis=1), 0.0)
+
+
+def first_finish(start, stop, scale, dy, strip, big, square, level):
+    mean = normalize(big, square, start, stop, 512)
+    for i in range(start, stop):
+        y = big[span(i, i + 1), :] * lax.rsqrt(1.0 + mean[span(i - start, i - start + 1)]) * scale
+        y = jnp.where(dy + (ROWS * strip - 3 + i) < EXTENT, y, 0.0)
+        level[span(i, i + 1), :] = y.astype(BF16)
+
+
+def second_multiply(start, stop, level, band_two, big):
     parts = []
     for g in range(2):
         lhs = jnp.concatenate(
-            [level[32 * a : 32 * a + 640, 256 * g : 256 * g + 256] for a in range(3)], axis=1
+            [level[span(start + a, stop + a), 256 * g : 256 * g + 256] for a in range(3)], axis=1
         )
         parts.append(dot_nt(lhs, band_two[g]))
-    big[0:640, 0:128] = parts[0][:, 0:128]
-    big[0:640, 128:256] = parts[0][:, 128:256] + parts[1][:, 0:128]
-    big[0:640, 256:384] = parts[1][:, 128:256]
-    normalize(big, square, mean, 20, 384)
-    dy, dx = as_column(offsets[0:1, :]), as_column(offsets[1:2, :])
+    big[span(start, stop), 0:128] = parts[0][:, 0:128]
+    big[span(start, stop), 128:256] = parts[0][:, 128:256] + parts[1][:, 0:128]
+    big[span(start, stop), 256:384] = parts[1][:, 128:256]
+
+
+def second_scale(gain, dx, block):
     placed = iota((SECS, 384), 1) // C + (BLOCK * block - 2)
     inside = (placed >= 0) & (placed < EXTENT) & (placed + dx >= 0) & (placed + dx < EXTENT)
-    scale = jnp.where(inside, jnp.concatenate([gain] * 3, axis=1), 0.0)
-
-    def finish(i, _):
-        at = pl.ds(pl.multiple_of(32 * i, 32), 32)
-        y = big[at, 0:384] * lax.rsqrt(1.0 + mean[at, 0:384]) * scale
+    return jnp.where(inside, jnp.concatenate([gain] * 3, axis=1), 0.0)
+
+
+def second_finish(start, stop, scale, dy, strip, big, square, columns):
+    mean = normalize(big, square, start, stop, 384)
+    for i in range(start, stop):
+        here = span(i, i + 1)
+        y = big[here, 0:384] * lax.rsqrt(1.0 + mean[span(i - start, i - start + 1)]) * scale
         row = ROWS * strip - 2 + i
-        y = jnp.where((dy + row >= 0) & (dy + row < EXTENT), y, 0.0)
-        y = jnp.where((row >= 0) & (row < EXTENT), y, 0.0)
+        inside = (dy + row >= 0) & (dy + row < EXTENT) & (row >= 0) & (row < EXTENT)
+        y = jnp.where(inside, y, 0.0)
         before, after = shift_sections(y, 384)
-        columns[at, 0:384] = before.astype(BF16)
-        columns[at, 384:768] = y.astype(BF16)
-        columns[at, 768:1152] = after.astype(BF16)
-        return 0
-
-    lax.fori_loop(0, 20, finish, 0, unroll=True)
-
-
-def third_layer(columns, band_three, strip, block, big, middle):
+        columns[here, 0:384] = before.astype(BF16)
+        columns[here, 384:768] = y.astype(BF16)
+        columns[here, 768:1152] = after.astype(BF16)
+
+
+def third_multiply(start, stop, columns, band_three, big):
     for g in range(2):
         total = None
         for b in range(3):
             for a in range(3):
-                lhs = columns[32 * b : 32 * b + 576, 384 * a + 128 * g : 384 * a + 128 * g + 256]
+                lhs = columns[span(start + b, stop + b), 384 * a + 128 * g : 384 * a + 128 * g + 256]
                 rhs = band_three[3 * b + a]
                 term = dot_nt(lhs, rhs if g else rhs[0:128])
                 total = term if total is None else total + term
         if g:
-            big[0:576, 128:384] = total
+            big[span(start, stop), 128:384] = total
         else:
-            big[0:576, 0:128] = total
+            big[span(start, stop), 0:128] = total
+
+
+def third_mask(block):
     lane = iota((SECS, 384), 1)
     column = jnp.where(lane < 320, lane, lane - 64) // C + (BLOCK * block - 1)
-    inside = (column >= 0) & (column < EXTENT)
+    return (column >= 0) & (column < EXTENT)
+
+
+def third_finish(start, stop, inside, strip, big, middle):
     low = iota((SECS, 128), 1) < 64
-
-    def finish(i, _):
-        at = pl.ds(pl.multiple_of(32 * i, 32), 32)
+    for i in range(start, stop):
         row = ROWS * strip - 1 + i
-        y = silu(big[at, 0:384])
+        y = silu(big[span(i, i + 1), 0:384])
         y = jnp.where(inside & (row >= 0) & (row < EXTENT), y, 0.0)
         before, after = shift_sections(y, 384)
-        middle[at, 0:256] = before[:, 0:256].astype(BF16)
-        middle[at, 256:512] = y[:, 0:256].astype(BF16)
-        middle[at, 512:768] = after[:, 0:256].astype(BF16)
-        middle[at, 768:896] = jnp.where(low, before[:, 256:384], y[:, 256:384]).astype(BF16)
-        middle[at, 896:1024] = after[:, 256:384].astype(BF16)
-        return 0
-
-    lax.fori_loop(0, 18, finish, 0, unroll=True)
-
-
-def fourth_layer(middle, band_four, big, out):
+        here = span(i, i + 1)
+        middle[here, 0:256] = before[:, 0:256].astype(BF16)
+        middle[here, 256:512] = y[:, 0:256].astype(BF16)
+        middle[here, 512:768] = after[:, 0:256].astype(BF16)
+        middle[here, 768:896] = jnp.where(low, before[:, 256:384], y[:, 256:384]).astype(BF16)
+        middle[here, 896:1024] = after[:, 256:384].astype(BF16)
+
+
+def fourth(start, stop, middle, band_four, out):
     total = None
     for b in range(3):
-        term = dot_nt(middle[32 * b : 32 * b + 512, :], band_four[b])
+        term = dot_nt(middle[span(start + b, stop + b), :], band_four[b])
         total = term if total is None else total + term
-    big[0:512, 0:256] = total
-    for i in range(ROWS):
-        out[:, i, :] = big[32 * i : 32 * i + 32, 0:256]
+    for i in range(start, stop):
+        out[:, i, :] = total[span(i - start, i - start + 1)]
+
+
+def layers(
+    recv, offsets, gain_one, gain_two, strip, block, band_one, band_two, band_three, band_four,
+    stage, lhs, big_one, big_two, big_three, square_one, square_two, level, columns, middle, out,
+):
+    gather_first(recv, stage, lhs)
+    dy, dx = as_column(offsets[0:1, :]), as_column(offsets[1:2, :])
+    scale_one, scale_two = first_scale(gain_one, dx, block), second_scale(gain_two, dx, block)
+    mask = third_mask(block)
+
+    def one(n):
+        first_finish(*FIRST[n : n + 2], scale_one, dy, strip, big_one, square_one, level)
+
+    def two(n):
+        second_finish(*SECOND[n : n + 2], scale_two, dy, strip, big_two, square_two, columns)
+
+    def three(n):
+        third_finish(*THIRD[n : n + 2], mask, strip, big_three, middle)
+
+    first_multiply(0, lhs, band_one, big_one)
+    first_multiply(1, lhs, band_one, big_one)
+    one(0)
+    second_multiply(*SECOND[0:2], level, band_two, big_two)
+    one(1)
+    second_multiply(*SECOND[1:3], level, band_two, big_two)
+    two(0)
+    two(1)
+    third_multiply(*THIRD[0:2], columns, band_three, big_three)
+    third_multiply(*THIRD[1:3], columns, band_three, big_three)
+    three(0)
+    three(1)
+    fourth(*FOURTH, middle, band_four, out)
 
 
 def kernel(
     raw_hbm, w_first_hbm, gain_one_hbm, w_second_hbm, gain_two_hbm, offsets_hbm, w_third_hbm,
     w_fourth_hbm, out,
     w_first, gain_one, w_second, gain_two, offsets, w_third, w_fourth, offsets_smem,
-    ext, send, recv, band_one, band_two, band_three, band_four, tile, wide, stage, lhs, big, square,
-    mean, level, columns, middle, load_sem, halo_send, halo_recv, pass_send, pass_recv,
+    ext, send, recv, band_one, band_two, band_three, band_four, tile, wide, stage, lhs, big_one,
+    big_two, big_three, square_one, square_two, level, columns, middle, load_sem, halo_send, halo_recv, pass_send, pass_recv,
 ):
     me, strip = lax.axis_index("sec"), lax.axis_index("strip")
     up = lax.rem(strip + STRIPS - 1, STRIPS)
@@ -365,10 +407,10 @@
     for copy in halos:
         copy.wait_send()
 
-    first_layer(recv, band_one, gain_a, offsets, strip, me, stage, lhs, big, square, mean, level)
-    second_layer(level, band_two, gain_b, offsets, strip, me, big, square, mean, columns)
-    third_layer(columns, band_three, strip, me, big, middle)
-    fourth_layer(middle, band_four, big, out)
+    layers(
+        recv, offsets, gain_a, gain_b, strip, me, band_one, band_two, band_three, band_four,
+        stage, lhs, big_one, big_two, big_three, square_one, square_two, level, columns, middle, out,
+    )
 
 
 def shards(raw_image, w_first, gain_one, w_second, gain_two, offsets, w_third, w_fourth):
@@ -399,8 +441,10 @@
             pltpu.VMEM((SECS * 16, 128), F32),
             pltpu.VMEM((352, 256), BF16),
             pltpu.VMEM((704, 512), F32),
+            pltpu.VMEM((640, 384), F32),
+            pltpu.VMEM((576, 384), F32),
             pltpu.VMEM((704, 512), BF16),
-            pltpu.VMEM((704, 512), F32),
+            pltpu.VMEM((640, 384), BF16),
             pltpu.VMEM((704, 512), BF16),
             pltpu.VMEM((640, 1152), BF16),
             pltpu.VMEM((576, 1024), BF16),
@@ -411,12 +455,17 @@
             pltpu.SemaphoreType.DMA,
         ],
         compiler_params=pltpu.CompilerParams(
-            collective_id=0, has_side_effects=True, vmem_limit_bytes=60 * 2**20
+            collective_id=0, has_side_effects=True, vmem_limit_bytes=48 * 2**20
         ),
         cost_estimate=pl.CostEstimate(flops=10**9, bytes_accessed=2**20, transcendentals=10**6),
     )(
-        raw_image.reshape(32, RAW), w_first, gain_one.reshape(1, C), w_second,
-        gain_two.reshape(1, C), offsets.T, w_third, w_fourth,
+        *[
+            pltpu.with_memory_space_constraint(x, pltpu.HBM)
+            for x in (
+                raw_image.reshape(32, RAW), w_first, gain_one.reshape(1, C), w_second,
+                gain_two.reshape(1, C), offsets.T, w_third, w_fourth,
+            )
+        ]
     )
     return result.reshape(1, SECS, ROWS, C * BLOCK)
 

time: 31.7 us -> 28.3 us (0.89)
  Pallas kernels: 29.6 us -> 27.4 us
  local copies, waits for them, and re-layouts: 1.87 us -> 0.8 us
    pallas_call x1, Pallas kernels: 29.6 us -> 27.4 us  [shards(): pl.pallas_call(kernel, out_shape=jax.ShapeDtypeStruct((SECS, ROWS, C * BL...]
    unnamed x1, local copies, waits for them, and re-layouts: 1.87 us -> 0.8 us
where the time goes in v3:
time: 28.3 us; the launch traced here: 28.2 us
  Pallas kernels  27.4 us (97%)
  local copies, waits for them, and re-layouts  0.8 us (3%)
    pallas_call x1, Pallas kernels, shards(): pl.pallas_call(kernel, out_shape=jax.ShapeDtypeStruct((SECS, ROWS, C * BL...  27.4 us
    unnamed x1, local copies, waits for them, and re-layouts  0.8 us

profile of v3, /device:TPU:25, one launch (start us, length us, event | category | flops | bytes accessed | tf_op | source)
XLA Modules:
  0.0 28.2 jit_solution(469528979971747717)
XLA Ops:
  0.0 27.4 %shard_map.82 = f32[32,16,256]{2,1,0:T(8,128)S(1)} custom-call(bf16[32,512]{1,0:T(8,128)(2,1)} %bitcast.6, bf16[9,32]{1,0:T(8,128)(2,1)} %w_first_hbm.1, f32[1,32]{1,0:T(1,128)} %bitcast.8, bf16[3,32,96]{2,1,0:T(8,128)(2,1)} %w_second_hbm.1, f32[1,32]{1,0:T(1,128)} %bitcast.9, s32[2,32]{1,0:T(2,128)} %bitcast.7, bf16[9,32,96]{2,1,0:T(8,128)(2,1)} %w_third_hbm.1, ...), custom_call_target="tpu_custom_call" | custom-call | flops 1000000000 | bytes 1048576 | tf_op jit(solution)/shard_map/pallas_call | solution.py:418
  27.4 0.8 %copy.10 = f32[1,32,16,256]{3,2,1,0:T(8,128)} copy(f32[1,32,16,256]{3,2,1,0:T(8,128)S(1)} %bitcast.5) | data formatting | bytes 1048576

commit v4 on v3

--- a/solution.py
+++ b/solution.py
@@ -25,6 +25,18 @@
 
 def peer_at(me, x, z):
     return lax.rem(me // 8 + x, 4) * 8 + lax.rem(lax.rem(me, 8) + z, 8)
+
+
+SEND_ORDER = sorted(range(SECS), key=lambda k: (k % 8, k // 8))
+
+
+def group_of(s):
+    return ((s % 8 + 2) % 8) // 4
+
+
+def slot_of(s):
+    x, z, g = s // 8, s % 8, group_of(s)
+    return 16 * g + 8 * (x // 2) + (z + 4 * ((x + g) % 2)) % 8
 
 
 def iota(shape, axis):
@@ -137,7 +149,7 @@
     return jnp.where(inside & (iota((64, 96), 1) - 32 == row), 1.0, 0.0).astype(BF16)
 
 
-def cut_windows(rows, dx, send):
+def cut_windows(rows, dx, send, start=lambda k: None):
     padded = jnp.concatenate([rows, jnp.zeros((64, 128), F32)], axis=1)
     shifted = pltpu.roll(padded, lax.rem(648 - 2 * dx, 640), 1)
     lane = iota((16, 128), 1)
@@ -160,41 +172,48 @@
                 then = jnp.where(even, pltpu.roll(pair[0], 96, 1), pair[1])
                 send[2 * group + odd] = here.astype(BF16)
                 send[2 * (group + 1) + odd] = then.astype(BF16)
-
-
-def as_column(row):
-    same = iota((SECS, SECS), 0) == iota((SECS, SECS), 1)
+        for k in SEND_ORDER[:4] if odd == 0 else SEND_ORDER[4:]:
+            start(k)
+
+
+def by_slot(row):
+    same = iota((SECS, SECS), 0) == slot_of(iota((SECS, SECS), 1))
     return jnp.sum(jnp.where(same, row.astype(F32), 0.0), axis=1, keepdims=True).astype(jnp.int32)
 
 
-FIRST, SECOND, THIRD, FOURTH = (0, 11, 22), (0, 9, 20), (0, 9, 18), (0, 16)
+THIRD, FOURTH = (0, 9, 18), (0, 16)
+HALF = SECS // 2
 
 
 def span(start, stop):
     return slice(32 * start, 32 * stop)
 
 
-def gather_first(recv, stage, lhs):
-    stage[...] = recv[...].reshape(SECS * 16, 128).astype(F32)
+def few(start, stop):
+    return slice(HALF * start, HALF * stop)
+
+
+def gather_first(recv, g, stage, lhs):
+    stage[g] = recv[few(g, g + 1)].reshape(HALF * 16, 128).astype(F32)
     for q in range(12):
-        piece = stage[pl.ds(q, SECS, stride=16), :].astype(BF16)
+        piece = stage[g, pl.ds(q, HALF, stride=16), :].astype(BF16)
         if q < 11:
-            lhs[32 * q : 32 * q + 32, 0:128] = piece
+            lhs[g, few(q, q + 1), 0:128] = piece
         if q > 0:
-            lhs[32 * q - 32 : 32 * q, 128:256] = piece
-
-
-def normalize(big, square, start, stop, lanes):
-    for i in range(start, stop):
-        v = silu(big[span(i, i + 1), 0:lanes])
-        big[span(i, i + 1), 0:lanes] = v
-        square[span(i, i + 1), 0:lanes] = (v * v).astype(BF16)
+            lhs[g, few(q - 1, q), 128:256] = piece
+
+
+def normalize(big, square, g, count, lanes):
+    for i in range(count):
+        v = silu(big[g, few(i, i + 1), :])
+        big[g, few(i, i + 1), :] = v
+        square[g, few(i, i + 1), :] = (v * v).astype(BF16)
     same = iota((256, 256), 0) // C == iota((256, 256), 1) // C
     spread = jnp.where(same, 1.0 / C, 0.0).astype(BF16)
     parts = []
     for low in range(0, lanes, 256):
         wide = min(256, lanes - low)
-        parts.append(dot_nn(square[span(start, stop), low : low + wide], spread[0:wide, 0:wide]))
+        parts.append(dot_nn(square[g, :, low : low + wide], spread[0:wide, 0:wide]))
     return jnp.concatenate(parts, axis=1)
 
 
@@ -205,52 +224,68 @@
     return before, after
 
 
-def first_multiply(half, lhs, band_one, big):
-    big[span(11 * half, 11 * half + 11), :] = dot_nn(lhs[...], band_one[half])
+def first_multiply(g, lhs, band_one, big):
+    for half in range(2):
+        big[g, few(11 * half, 11 * half + 11), :] = dot_nn(lhs[g], band_one[half])
 
 
 def first_scale(gain, dx, block):
-    lane = iota((SECS, 512), 1)
+    lane = iota((HALF, 512), 1)
     column = 6 * (lane // 256) + (lane % 256) // 32
     inside = column + dx + (BLOCK * block - 3) < EXTENT
     return jnp.where(inside, jnp.concatenate([gain] * 4, axis=1), 0.0)
 
 
-def first_finish(start, stop, scale, dy, strip, big, square, level):
-    mean = normalize(big, square, start, stop, 512)
-    for i in range(start, stop):
-        y = big[span(i, i + 1), :] * lax.rsqrt(1.0 + mean[span(i - start, i - start + 1)]) * scale
+def first_finish(g, scale, dy, strip, big, square, level):
+    mean = normalize(big, square, g, 22, 512)
+    for i in range(22):
+        here = few(i, i + 1)
+        y = big[g, here, :] * lax.rsqrt(1.0 + mean[here]) * scale
         y = jnp.where(dy + (ROWS * strip - 3 + i) < EXTENT, y, 0.0)
-        level[span(i, i + 1), :] = y.astype(BF16)
-
-
-def second_multiply(start, stop, level, band_two, big):
+        level[g, here, :] = y.astype(BF16)
+
+
+def second_multiply(g, level, band_two, big):
     parts = []
-    for g in range(2):
+    for side in range(2):
         lhs = jnp.concatenate(
-            [level[span(start + a, stop + a), 256 * g : 256 * g + 256] for a in range(3)], axis=1
+            [level[g, few(a, a + 20), 256 * side : 256 * side + 256] for a in range(3)], axis=1
         )
-        parts.append(dot_nt(lhs, band_two[g]))
-    big[span(start, stop), 0:128] = parts[0][:, 0:128]
-    big[span(start, stop), 128:256] = parts[0][:, 128:256] + parts[1][:, 0:128]
-    big[span(start, stop), 256:384] = parts[1][:, 128:256]
+        parts.append(dot_nt(lhs, band_two[side]))
+    big[g, :, 0:128] = parts[0][:, 0:128]
+    big[g, :, 128:256] = parts[0][:, 128:256] + parts[1][:, 0:128]
+    big[g, :, 256:384] = parts[1][:, 128:256]
 
 
 def second_scale(gain, dx, block):
-    placed = iota((SECS, 384), 1) // C + (BLOCK * block - 2)
+    placed = iota((HALF, 384), 1) // C + (BLOCK * block - 2)
     inside = (placed >= 0) & (placed < EXTENT) & (placed + dx >= 0) & (placed + dx < EXTENT)
     return jnp.where(inside, jnp.concatenate([gain] * 3, axis=1), 0.0)
 
 
-def second_finish(start, stop, scale, dy, strip, big, square, columns):
-    mean = normalize(big, square, start, stop, 384)
-    for i in range(start, stop):
-        here = span(i, i + 1)
-        y = big[here, 0:384] * lax.rsqrt(1.0 + mean[span(i - start, i - start + 1)]) * scale
+def second_finish(g, scale, dy, strip, big, square):
+    mean = normalize(big, square, g, 20, 384)
+    for i in range(20):
+        here = few(i, i + 1)
+        y = big[g, here, :] * lax.rsqrt(1.0 + mean[here]) * scale
         row = ROWS * strip - 2 + i
         inside = (dy + row >= 0) & (dy + row < EXTENT) & (row >= 0) & (row < EXTENT)
-        y = jnp.where(inside, y, 0.0)
+        big[g, here, :] = jnp.where(inside, y, 0.0)
+
+
+def merge(big, columns):
+    pos = iota((8, 384), 0)
+    outer = (pos < 2) | (pos >= 6)
+    for i in range(20):
+        tiles = []
+        for t in range(2):
+            at = slice(HALF * i + 8 * t, HALF * i + 8 * t + 8)
+            a, b = big[0, at, :], big[1, at, :]
+            tiles.append(jnp.where(outer, a, pltpu.roll(b, 4, 0)))
+            tiles.append(jnp.where(outer, pltpu.roll(a, 4, 0), b))
+        y = jnp.concatenate(tiles, axis=0)
         before, after = shift_sections(y, 384)
+        here = span(i, i + 1)
         columns[here, 0:384] = before.astype(BF16)
         columns[here, 384:768] = y.astype(BF16)
         columns[here, 768:1152] = after.astype(BF16)
@@ -302,35 +337,26 @@
 
 
 def layers(
-    recv, offsets, gain_one, gain_two, strip, block, band_one, band_two, band_three, band_four,
-    stage, lhs, big_one, big_two, big_three, square_one, square_two, level, columns, middle, out,
+    arrived, recv, offsets, gain_one, gain_two, strip, block, band_one, band_two, band_three,
+    band_four, stage, lhs, big_one, big_two, big_three, square_one, square_two, level, columns,
+    middle, out,
 ):
-    gather_first(recv, stage, lhs)
-    dy, dx = as_column(offsets[0:1, :]), as_column(offsets[1:2, :])
-    scale_one, scale_two = first_scale(gain_one, dx, block), second_scale(gain_two, dx, block)
+    dys, dxs = by_slot(offsets[0:1, :]), by_slot(offsets[1:2, :])
     mask = third_mask(block)
-
-    def one(n):
-        first_finish(*FIRST[n : n + 2], scale_one, dy, strip, big_one, square_one, level)
-
-    def two(n):
-        second_finish(*SECOND[n : n + 2], scale_two, dy, strip, big_two, square_two, columns)
-
-    def three(n):
-        third_finish(*THIRD[n : n + 2], mask, strip, big_three, middle)
-
-    first_multiply(0, lhs, band_one, big_one)
-    first_multiply(1, lhs, band_one, big_one)
-    one(0)
-    second_multiply(*SECOND[0:2], level, band_two, big_two)
-    one(1)
-    second_multiply(*SECOND[1:3], level, band_two, big_two)
-    two(0)
-    two(1)
+    for g in range(2):
+        dy, dx = dys[few(g, g + 1)], dxs[few(g, g + 1)]
+        scale_one, scale_two = first_scale(gain_one, dx, block), second_scale(gain_two, dx, block)
+        arrived(g)
+        gather_first(recv, g, stage, lhs)
+        first_multiply(g, lhs, band_one, big_one)
+        first_finish(g, scale_one, dy, strip, big_one, square_one, level)
+        second_multiply(g, level, band_two, big_two)
+        second_finish(g, scale_two, dy, strip, big_two, square_two)
+    merge(big_two, columns)
     third_multiply(*THIRD[0:2], columns, band_three, big_three)
     third_multiply(*THIRD[1:3], columns, band_three, big_three)
-    three(0)
-    three(1)
+    third_finish(*THIRD[0:2], mask, strip, big_three, middle)
+    third_finish(*THIRD[1:3], mask, strip, big_three, middle)
     fourth(*FOURTH, middle, band_four, out)
 
 
@@ -390,27 +416,35 @@
     chosen = pick_rows(strip, dy)
     for copy in halos:
         copy.wait_recv()
-    cut_windows(dot_nn(chosen, ext[...]), dx, send)
-
-    for x, z in PEERS:
-        peer = peer_at(me, x, z)
-        pltpu.make_async_remote_copy(
-            src_ref=send.at[peer], dst_ref=recv.at[me], send_sem=pass_send, recv_sem=pass_recv,
-            device_id={"sec": peer}, device_id_type=MESH_ID,
-        ).start()
-    recv[me] = send[me]
+    slot, group = slot_of(me), group_of(me)
+
+    def start(k):
+        @pl.when(me != k)
+        def _():
+            pltpu.make_async_remote_copy(
+                src_ref=send.at[k], dst_ref=recv.at[slot], send_sem=pass_send,
+                recv_sem=pass_recv.at[group], device_id={"sec": k}, device_id_type=MESH_ID,
+            ).start()
+
+    cut_windows(dot_nn(chosen, ext[...]), dx, send, start)
+    pltpu.make_async_copy(send.at[me], recv.at[slot], pass_recv.at[group]).start()
     build_third(w_third, wide, band_three)
     build_fourth(w_fourth, wide, band_four)
     gain_a, gain_b = build_gain(gain_one, tile), build_gain(gain_two, tile)
-    pltpu.make_async_copy(send.at[0 : SECS - 1], recv.at[0 : SECS - 1], pass_recv).wait()
+
+    def arrived(g):
+        pltpu.make_async_copy(
+            send.at[0:HALF], recv.at[HALF * g : HALF * g + HALF], pass_recv.at[g]
+        ).wait()
+
+    layers(
+        arrived, recv, offsets, gain_a, gain_b, strip, me, band_one, band_two, band_three,
+        band_four, stage, lhs, big_one, big_two, big_three, square_one, square_two, level, columns,
+        middle, out,
+    )
     pltpu.make_async_copy(send.at[0 : SECS - 1], recv.at[0 : SECS - 1], pass_send).wait()
     for copy in halos:
         copy.wait_send()
-
-    layers(
-        recv, offsets, gain_a, gain_b, strip, me, band_one, band_two, band_three, band_four,
-        stage, lhs, big_one, big_two, big_three, square_one, square_two, level, columns, middle, out,
-    )
 
 
 def shards(raw_image, w_first, gain_one, w_second, gain_two, offsets, w_third, w_fourth):
@@ -438,21 +472,21 @@
             pltpu.VMEM((3, 256, 1024), BF16),
             pltpu.VMEM((16, 128), F32),
             pltpu.VMEM((C, 256), F32),
-            pltpu.VMEM((SECS * 16, 128), F32),
-            pltpu.VMEM((352, 256), BF16),
-            pltpu.VMEM((704, 512), F32),
-            pltpu.VMEM((640, 384), F32),
+            pltpu.VMEM((2, HALF * 16, 128), F32),
+            pltpu.VMEM((2, 11 * HALF, 256), BF16),
+            pltpu.VMEM((2, 22 * HALF, 512), F32),
+            pltpu.VMEM((2, 20 * HALF, 384), F32),
             pltpu.VMEM((576, 384), F32),
-            pltpu.VMEM((704, 512), BF16),
-            pltpu.VMEM((640, 384), BF16),
-            pltpu.VMEM((704, 512), BF16),
+            pltpu.VMEM((2, 22 * HALF, 512), BF16),
+            pltpu.VMEM((2, 20 * HALF, 384), BF16),
+            pltpu.VMEM((2, 22 * HALF, 512), BF16),
             pltpu.VMEM((640, 1152), BF16),
             pltpu.VMEM((576, 1024), BF16),
             pltpu.SemaphoreType.DMA((9,)),
             pltpu.SemaphoreType.DMA((2,)),
             pltpu.SemaphoreType.DMA((2,)),
             pltpu.SemaphoreType.DMA,
-            pltpu.SemaphoreType.DMA,
+            pltpu.SemaphoreType.DMA((2,)),
         ],
         compiler_params=pltpu.CompilerParams(
             collective_id=0, has_side_effects=True, vmem_limit_bytes=48 * 2**20

time: 28.3 us -> 27.3 us (0.965)
  Pallas kernels: 27.4 us -> 26.4 us
    pallas_call x1, Pallas kernels: 27.4 us -> 26.4 us  [shards(): pl.pallas_call(kernel, out_shape=jax.ShapeDtypeStruct((SECS, ROWS, C * BL...]
where the time goes in v4:
time: 27.3 us; the launch traced here: 27.2 us
  Pallas kernels  26.4 us (97%)
  local copies, waits for them, and re-layouts  0.8 us (3%)
    pallas_call x1, Pallas kernels, shards(): pl.pallas_call(kernel, out_shape=jax.ShapeDtypeStruct((SECS, ROWS, C * BL...  26.4 us
    unnamed x1, local copies, waits for them, and re-layouts  0.8 us

profile of v4, /device:TPU:25, one launch (start us, length us, event | category | flops | bytes accessed | tf_op | source)
XLA Modules:
  0.0 27.2 jit_solution(535048371526128868)
XLA Ops:
  0.0 26.4 %shard_map.82 = f32[32,16,256]{2,1,0:T(8,128)S(1)} custom-call(bf16[32,512]{1,0:T(8,128)(2,1)} %bitcast.6, bf16[9,32]{1,0:T(8,128)(2,1)} %w_first_hbm.1, f32[1,32]{1,0:T(1,128)} %bitcast.8, bf16[3,32,96]{2,1,0:T(8,128)(2,1)} %w_second_hbm.1, f32[1,32]{1,0:T(1,128)} %bitcast.9, s32[2,32]{1,0:T(2,128)} %bitcast.7, bf16[9,32,96]{2,1,0:T(8,128)(2,1)} %w_third_hbm.1, ...), custom_call_target="tpu_custom_call" | custom-call | flops 1000000000 | bytes 1048576 | tf_op jit(solution)/shard_map/pallas_call | solution.py:452
  26.4 0.8 %copy.10 = f32[1,32,16,256]{3,2,1,0:T(8,128)} copy(f32[1,32,16,256]{3,2,1,0:T(8,128)S(1)} %bitcast.5) | data formatting | bytes 1048576

commit v5 on v4

--- a/solution.py
+++ b/solution.py
@@ -149,9 +149,12 @@
     return jnp.where(inside & (iota((64, 96), 1) - 32 == row), 1.0, 0.0).astype(BF16)
 
 
-def cut_windows(rows, dx, send, start=lambda k: None):
-    padded = jnp.concatenate([rows, jnp.zeros((64, 128), F32)], axis=1)
-    shifted = pltpu.roll(padded, lax.rem(648 - 2 * dx, 640), 1)
+def shift_columns(rows, dx):
+    padded = jnp.concatenate([rows.astype(F32), jnp.zeros((32, 128), F32)], axis=1)
+    return pltpu.roll(padded, lax.rem(648 - 2 * dx, 640), 1).astype(BF16)
+
+
+def cut_windows(shifted, send, start=lambda k: None):
     lane = iota((16, 128), 1)
     low = (lane // 64) == 0
     even = (lane // 32) % 2 == 0
@@ -364,7 +367,7 @@
     raw_hbm, w_first_hbm, gain_one_hbm, w_second_hbm, gain_two_hbm, offsets_hbm, w_third_hbm,
     w_fourth_hbm, out,
     w_first, gain_one, w_second, gain_two, offsets, w_third, w_fourth, offsets_smem,
-    ext, send, recv, band_one, band_two, band_three, band_four, tile, wide, stage, lhs, big_one,
+    raw, ext, send, recv, band_one, band_two, band_three, band_four, tile, wide, stage, lhs, big_one,
     big_two, big_three, square_one, square_two, level, columns, middle, load_sem, halo_send, halo_recv, pass_send, pass_recv,
 ):
     me, strip = lax.axis_index("sec"), lax.axis_index("strip")
@@ -375,7 +378,7 @@
         pltpu.make_async_copy(source, target, load_sem.at[n])
         for n, (source, target) in enumerate(
             (
-                (raw_hbm, ext.at[32:64, :]),
+                (raw_hbm, raw),
                 (offsets_hbm, offsets_smem),
                 (w_first_hbm, w_first),
                 (w_second_hbm, w_second),
@@ -399,6 +402,8 @@
 
     for load in loads:
         load.wait()
+    dy, dx = offsets_smem[0, me], offsets_smem[1, me]
+    ext[32:64, :] = shift_columns(raw[...], dx)
     pl.semaphore_wait(barrier, SECS + 1)
 
     halos = []
@@ -412,7 +417,6 @@
         halos.append(copy)
     build_first(w_first, tile, band_one)
     build_second(w_second, wide, band_two)
-    dy, dx = offsets_smem[0, me], offsets_smem[1, me]
     chosen = pick_rows(strip, dy)
     for copy in halos:
         copy.wait_recv()
@@ -426,7 +430,7 @@
                 recv_sem=pass_recv.at[group], device_id={"sec": k}, device_id_type=MESH_ID,
             ).start()
 
-    cut_windows(dot_nn(chosen, ext[...]), dx, send, start)
+    cut_windows(dot_nn(chosen, ext[...]), send, start)
     pltpu.make_async_copy(send.at[me], recv.at[slot], pass_recv.at[group]).start()
     build_third(w_third, wide, band_three)
     build_fourth(w_fourth, wide, band_four)
@@ -463,7 +467,8 @@
             pltpu.VMEM((9, C, 96), BF16),
             pltpu.VMEM((9, C, 96), BF16),
             pltpu.SMEM((2, SECS), jnp.int32),
-            pltpu.VMEM((96, RAW), BF16),
+            pltpu.VMEM((32, RAW), BF16),
+            pltpu.VMEM((96, RAW + 128), BF16),
             pltpu.VMEM((SECS, 16, 128), BF16),
             pltpu.VMEM((SECS, 16, 128), BF16),
             pltpu.VMEM((2, 256, 512), BF16),

time: 27.3 us -> 27.3 us (level)
  no operation moved by 1% of the time
where the time goes in v5:
time: 27.3 us; the launch traced here: 27.2 us
  Pallas kernels  26.4 us (97%)
  local copies, waits for them, and re-layouts  0.8 us (3%)
    pallas_call x1, Pallas kernels, shards(): pl.pallas_call(kernel, out_shape=jax.ShapeDtypeStruct((SECS, ROWS, C * BL...  26.4 us
    unnamed x1, local copies, waits for them, and re-layouts  0.8 us

profile of v5, /device:TPU:25, one launch (start us, length us, event | category | flops | bytes accessed | tf_op | source)
XLA Modules:
  0.0 27.2 jit_solution(6283922814451678475)
XLA Ops:
  0.0 26.4 %shard_map.82 = f32[32,16,256]{2,1,0:T(8,128)S(1)} custom-call(bf16[32,512]{1,0:T(8,128)(2,1)} %bitcast.6, bf16[9,32]{1,0:T(8,128)(2,1)} %w_first_hbm.1, f32[1,32]{1,0:T(1,128)} %bitcast.8, bf16[3,32,96]{2,1,0:T(8,128)(2,1)} %w_second_hbm.1, f32[1,32]{1,0:T(1,128)} %bitcast.9, s32[2,32]{1,0:T(2,128)} %bitcast.7, bf16[9,32,96]{2,1,0:T(8,128)(2,1)} %w_third_hbm.1, ...), custom_call_target="tpu_custom_call" | custom-call | flops 1000000000 | bytes 1048576 | tf_op jit(solution)/shard_map/pallas_call | solution.py:456
  26.4 0.8 %copy.10 = f32[1,32,16,256]{3,2,1,0:T(8,128)} copy(f32[1,32,16,256]{3,2,1,0:T(8,128)S(1)} %bitcast.5) | data formatting | bytes 1048576
